TPU v7x, 32 devices: a whole 2x2x4 slice. The times are simulated.
32 devices in a mesh: batch: 4 (over y, x), ctx: 8 (over z, core).
Axes of the slice: x: 2, y: 2, z: 4, core: 2. Of those that a mesh axis runs over, the one named last changes fastest.
Arguments:
- inputs: bfloat16 [8, 1024, 768], P('batch', 'ctx'), may hold values from -6 to 6
- cotangent: bfloat16 [8, 1024, 768], P('batch', 'ctx'), may hold values from -6 to 6
- lengths: int32 [8, 4], P('batch'), may hold values from 1 to 640, 1024 in all within a row
- qkv_weight: float32 [2304, 768], P(('batch', 'ctx')), may hold values from -0.3125 to 0.3125
- qkv_moment: float32 [2304, 768], P(('batch', 'ctx')), may hold values from -32 to 32
- qkv_square: float32 [2304, 768], P(('batch', 'ctx')), may hold values from 106.496 to 434.176
- out_weight: float32 [768, 768], P(('batch', 'ctx')), may hold values from -0.3125 to 0.3125
- out_moment: float32 [768, 768], P(('batch', 'ctx')), may hold values from -20 to 20
- out_square: float32 [768, 768], P(('batch', 'ctx')), may hold values from 81.92 to 409.6
- fc_weight: float32 [3072, 768], P(('batch', 'ctx')), may hold values from -0.21875 to 0.21875
- fc_moment: float32 [3072, 768], P(('batch', 'ctx')), may hold values from -16 to 16
- fc_square: float32 [3072, 768], P(('batch', 'ctx')), may hold values from 38.5024 to 155.648
- proj_weight: float32 [3072, 768], P(('batch', 'ctx')), may hold values from -0.109375 to 0.109375
- proj_moment: float32 [3072, 768], P(('batch', 'ctx')), may hold values from -32 to 32
- proj_square: float32 [3072, 768], P(('batch', 'ctx')), may hold values from 155.648 to 622.592
- vectors: float32 [12, 768], P(None, ('batch', 'ctx')), may hold values from -1.2 to 2.2
- vectors_moment: float32 [12, 768], P(None, ('batch', 'ctx')), may hold values from -64 to 64
- vectors_square: float32 [12, 768], P(None, ('batch', 'ctx')), may hold values from 434.176 to 1720.32
Outputs:
- layer_out: bfloat16 [8, 1024, 768], P('batch', 'ctx')
- input_grad: bfloat16 [8, 1024, 768], P('batch', 'ctx')
- qkv_grad: float32 [2304, 768], P(('batch', 'ctx'))
- qkv_moment_new: float32 [2304, 768], P(('batch', 'ctx'))
- qkv_square_new: float32 [2304, 768], P(('batch', 'ctx'))
- qkv_weight_new: float32 [2304, 768], P(('batch', 'ctx'))
- out_grad: float32 [768, 768], P(('batch', 'ctx'))
- out_moment_new: float32 [768, 768], P(('batch', 'ctx'))
- out_square_new: float32 [768, 768], P(('batch', 'ctx'))
- out_weight_new: float32 [768, 768], P(('batch', 'ctx'))
- fc_grad: float32 [3072, 768], P(('batch', 'ctx'))
- fc_moment_new: float32 [3072, 768], P(('batch', 'ctx'))
- fc_square_new: float32 [3072, 768], P(('batch', 'ctx'))
- fc_weight_new: float32 [3072, 768], P(('batch', 'ctx'))
- proj_grad: float32 [3072, 768], P(('batch', 'ctx'))
- proj_moment_new: float32 [3072, 768], P(('batch', 'ctx'))
- proj_square_new: float32 [3072, 768], P(('batch', 'ctx'))
- proj_weight_new: float32 [3072, 768], P(('batch', 'ctx'))
- vectors_grad: float32 [12, 768], P(None, ('batch', 'ctx'))
- vectors_moment_new: float32 [12, 768], P(None, ('batch', 'ctx'))
- vectors_square_new: float32 [12, 768], P(None, ('batch', 'ctx'))
- vectors_new: float32 [12, 768], P(None, ('batch', 'ctx'))
Inputs may be any that keep to these rules, and one draw needn't show every extreme that they name: Each row holds 4 document lengths that sum to 1024; the longest is exactly 640.
All inputs are finite; a program needn't handle non-finite values.
Results may differ from a plain program's by a relative error of at most 0.017.
The roundings to bfloat16 on the way count: a program that leaves them out, or rounds other values in their place, can miss the bound.
Values may be sent and summed in bfloat16 or wider, within the bound.
A program may use at most 256 MiB of HBM per device.

v0:
```python
import math

import jax
import jax.numpy as jnp
from jax import lax
from jax.sharding import PartitionSpec as P

H = 12
HD = 64
STEP = 10


norm_eps = 1e-05
beta_one = 0.9
beta_two = 0.95
adam_eps = 1e-08
rate_matrix = 0.1
rate_vector = 0.6
decay_matrix = 0.1
score_scale = 0.125
masked_score = -1e30


def norm_layer(values, norm_gain, norm_bias):
    center = values - jnp.mean(values, axis=-1, keepdims=True)
    spread = jnp.mean(center * center, axis=-1, keepdims=True)
    return center * lax.rsqrt(spread + norm_eps) * norm_gain + norm_bias


def gelu_tanh(values):
    return jax.nn.gelu(values, approximate=True)


def natural_positions(row_index, seq_rows, ctx_count):
    device = row_index // seq_rows
    within = row_index % seq_rows
    half_rows = seq_rows // 2
    block_id = jnp.where(within < half_rows, device, 2 * ctx_count - 1 - device)
    return block_id * half_rows + within % half_rows


def document_ids(positions, seq_lengths):
    bounds = jnp.cumsum(seq_lengths, axis=1)[:, :-1]
    return jnp.sum((positions[None, :, None] >= bounds[:, None, :]).astype(jnp.int32), axis=2)


def dot_rows(left, right):
    return lax.dot_general(
        left, right, (((1,), (1,)), ((), ())), preferred_element_type=jnp.float32
    )


def dot_cols(left, right):
    return lax.dot_general(
        left, right, (((0,), (0,)), ((), ())), preferred_element_type=jnp.float32
    )


def split_heads(array):
    return array.reshape(array.shape[0], array.shape[1], H, HD)


def adam_update(weight, moment, square, gradient, rate, decay):
    moment_new = beta_one * moment + (1.0 - beta_one) * gradient
    square_new = beta_two * square + (1.0 - beta_two) * gradient * gradient
    corrected = moment_new / (1.0 - beta_one**STEP)
    scaled = square_new / (1.0 - beta_two**STEP)
    weight_new = weight - rate * (corrected / (jnp.sqrt(scaled) + adam_eps) + decay * weight)
    return (moment_new, square_new, weight_new)


def score_block(query_part, key_part, query_pos, query_doc, key_pos, key_doc):
    scores = (
        jnp.einsum(
            "bqhd,bkhd->bhqk",
            split_heads(query_part),
            split_heads(key_part),
            preferred_element_type=jnp.float32,
        )
        * score_scale
    )
    allowed = (key_pos[None, None, None, :] <= query_pos[None, None, :, None]) & (
        key_doc[:, None, None, :] == query_doc[:, None, :, None]
    )
    return (jnp.where(allowed, scores, masked_score), allowed)


def probabilities(query_part, key_part, query_pos, query_doc, key_pos, key_doc, lse_part):
    scores, allowed = score_block(query_part, key_part, query_pos, query_doc, key_pos, key_doc)
    return jnp.where(allowed, jnp.exp(scores - jnp.transpose(lse_part, (0, 2, 1))[..., None]), 0.0)


def score_grads(shares, grad_part, value_part, delta_part):
    grad_shares = jnp.einsum(
        "bqhd,bkhd->bhqk",
        split_heads(grad_part),
        split_heads(value_part),
        preferred_element_type=jnp.float32,
    )
    return (shares * (grad_shares - jnp.transpose(delta_part, (0, 2, 1))[..., None])).astype(
        jnp.bfloat16
    )


def local(
    inputs,
    cotangent,
    lengths,
    qkv_weight,
    qkv_moment,
    qkv_square,
    out_weight,
    out_moment,
    out_square,
    fc_weight,
    fc_moment,
    fc_square,
    proj_weight,
    proj_moment,
    proj_square,
    vectors,
    vectors_moment,
    vectors_square,
):
    groups, rows_seq, model_width = inputs.shape
    total_rows = groups * rows_seq
    ctx_count = lax.axis_size("ctx")
    local_index = lax.axis_index("ctx") * rows_seq + jnp.arange(rows_seq, dtype=jnp.int32)
    query_pos = natural_positions(local_index, rows_seq, ctx_count)
    query_doc = document_ids(query_pos, lengths)

    def block_places(first_row, count_rows):
        positions = natural_positions(
            first_row + jnp.arange(count_rows, dtype=jnp.int32), rows_seq, ctx_count
        )
        return (positions, document_ids(positions, lengths))

    qkv_low = qkv_weight.astype(jnp.bfloat16)
    out_low = out_weight.astype(jnp.bfloat16)
    fc_low = fc_weight.astype(jnp.bfloat16)
    proj_low = proj_weight.astype(jnp.bfloat16)
    qkv_full, out_full, vector_full = (
        lax.all_gather(qkv_low, ("batch", "ctx"), axis=0, tiled=True),
        lax.all_gather(out_low, ("batch", "ctx"), axis=0, tiled=True),
        lax.all_gather(vectors.astype(jnp.bfloat16), ("batch", "ctx"), axis=1, tiled=True),
    )
    vector_rows = vector_full.astype(jnp.float32)
    tokens = inputs.reshape(total_rows, model_width).astype(jnp.float32)
    hidden_one_low = norm_layer(tokens, vector_rows[0], vector_rows[1]).astype(jnp.bfloat16)
    bias_qkv = jnp.concatenate(
        [vector_rows[2], jnp.zeros((model_width,), jnp.float32), vector_rows[3]]
    )
    mixed_low = (dot_rows(hidden_one_low, qkv_full) + bias_qkv).astype(jnp.bfloat16)
    queries = mixed_low[:, :model_width].reshape(groups, rows_seq, model_width)
    key_rows = mixed_low[:, model_width : 2 * model_width].reshape(groups, rows_seq, model_width)
    value_rows = mixed_low[:, 2 * model_width :].reshape(groups, rows_seq, model_width)
    start_state = (
        jnp.zeros((groups, H, rows_seq, HD), jnp.float32),
        jnp.full((groups, H, rows_seq), masked_score, jnp.float32),
        jnp.zeros((groups, H, rows_seq), jnp.float32),
    )
    key_piece = lax.all_gather(key_rows, "ctx", axis=1, tiled=True)
    value_piece = lax.all_gather(value_rows, "ctx", axis=1, tiled=True)
    piece_rows = key_piece.shape[1]
    sub_rows = math.gcd(piece_rows, 128)

    def forward_inner_step(block_turn, state_now):
        accum_out, run_max, run_sum = state_now
        offset = block_turn * sub_rows
        key_part = lax.dynamic_slice_in_dim(key_piece, offset, sub_rows, 1)
        value_part = lax.dynamic_slice_in_dim(value_piece, offset, sub_rows, 1)
        key_pos, key_doc = block_places(offset, sub_rows)
        scores, allowed = score_block(queries, key_part, query_pos, query_doc, key_pos, key_doc)
        new_max = jnp.maximum(run_max, jnp.max(scores, axis=-1))
        factor = jnp.exp(run_max - new_max)
        weights = jnp.where(allowed, jnp.exp(scores - new_max[..., None]), 0.0)
        run_sum = run_sum * factor + jnp.sum(weights, axis=-1)
        added = jnp.einsum(
            "bhqk,bkhd->bhqd",
            weights.astype(jnp.bfloat16),
            split_heads(value_part),
            preferred_element_type=jnp.float32,
        )
        return (accum_out * factor[..., None] + added, new_max, run_sum)

    accum_out, run_max, run_sum = lax.fori_loop(
        0, piece_rows // sub_rows, forward_inner_step, start_state
    )
    attended_f = jnp.transpose(accum_out / run_sum[..., None], (0, 2, 1, 3)).reshape(
        groups, rows_seq, model_width
    )
    log_sum = jnp.transpose(run_max + jnp.log(run_sum), (0, 2, 1))
    attended_low = attended_f.astype(jnp.bfloat16).reshape(total_rows, model_width)
    middle = (
        tokens
        + jnp.dot(attended_low, out_full, preferred_element_type=jnp.float32)
        + vector_rows[4]
    )
    hidden_two_low = norm_layer(middle, vector_rows[5], vector_rows[6]).astype(jnp.bfloat16)
    bias_fc = vector_rows[8:].reshape(-1)
    pieces = lax.all_gather(fc_low, ("batch", "ctx"), axis=0, tiled=True)
    count_rows = pieces.shape[0]
    before = dot_rows(hidden_two_low, pieces) + bias_fc
    active_low = gelu_tanh(before).astype(jnp.bfloat16)
    column_part = active_low
    mlp_out = jnp.dot(
        column_part,
        lax.all_gather(proj_low, ("batch", "ctx"), axis=0, tiled=True),
        preferred_element_type=jnp.float32,
    )
    layer_out = (
        (middle + mlp_out + vector_rows[7])
        .astype(jnp.bfloat16)
        .reshape(groups, rows_seq, model_width)
    )
    grad_top = cotangent.reshape(total_rows, model_width)
    grad_top_f = grad_top.astype(jnp.float32)
    proj_grad = lax.psum_scatter(
        dot_cols(active_low, grad_top), ("batch", "ctx"), scatter_dimension=0, tiled=True
    )
    grad_active = dot_rows(grad_top, lax.all_gather(proj_low, ("batch", "ctx"), axis=0, tiled=True))
    column_part = before
    unused, pullback = jax.vjp(gelu_tanh, column_part)
    grad_before = pullback(grad_active)[0].astype(jnp.bfloat16)
    fc_grad = lax.psum_scatter(
        dot_cols(grad_before, hidden_two_low), ("batch", "ctx"), scatter_dimension=0, tiled=True
    )
    column_part = grad_before
    grad_hidden_two = jnp.dot(
        column_part,
        lax.all_gather(fc_low, ("batch", "ctx"), axis=0, tiled=True),
        preferred_element_type=jnp.float32,
    )
    unused, pull_two = jax.vjp(norm_layer, middle, vector_rows[5], vector_rows[6])
    grad_middle_norm, grad_gain_two, grad_bias_two = pull_two(grad_hidden_two)
    grad_middle = grad_top_f + grad_middle_norm
    grad_middle_low = grad_middle.astype(jnp.bfloat16)
    out_term = dot_cols(attended_low, grad_middle_low)
    qkv_back, out_back = (
        lax.all_gather(qkv_low, ("batch", "ctx"), axis=0, tiled=True),
        lax.all_gather(out_low, ("batch", "ctx"), axis=0, tiled=True),
    )
    grad_attended = (
        dot_rows(grad_middle_low, out_back)
        .astype(jnp.bfloat16)
        .reshape(groups, rows_seq, model_width)
    )
    delta_rows = jnp.sum(split_heads(grad_attended.astype(jnp.float32) * attended_f), axis=-1)
    head_zeros = jnp.zeros((groups, rows_seq, H, HD), jnp.float32)
    lse_whole, delta_whole = (
        lax.all_gather(log_sum, "ctx", axis=1, tiled=True),
        lax.all_gather(delta_rows, "ctx", axis=1, tiled=True),
    )
    query_key_piece = lax.all_gather(key_rows, "ctx", axis=1, tiled=True)
    query_value_piece = lax.all_gather(value_rows, "ctx", axis=1, tiled=True)
    piece_rows = query_key_piece.shape[1]
    query_sub_rows = math.gcd(piece_rows, 128)

    def query_inner_step(block_turn, state_now):
        offset = block_turn * query_sub_rows
        key_part = lax.dynamic_slice_in_dim(query_key_piece, offset, query_sub_rows, 1)
        value_part = lax.dynamic_slice_in_dim(query_value_piece, offset, query_sub_rows, 1)
        key_pos, key_doc = block_places(offset, query_sub_rows)
        shares = probabilities(queries, key_part, query_pos, query_doc, key_pos, key_doc, log_sum)
        grad_scores = score_grads(shares, grad_attended, value_part, delta_rows)
        return state_now + score_scale * jnp.einsum(
            "bhqk,bkhd->bqhd",
            grad_scores,
            split_heads(key_part),
            preferred_element_type=jnp.float32,
        )

    grad_queries = lax.fori_loop(0, piece_rows // query_sub_rows, query_inner_step, head_zeros)
    query_piece = lax.all_gather(queries, "ctx", axis=1, tiled=True)
    grad_piece = lax.all_gather(grad_attended, "ctx", axis=1, tiled=True)
    piece_rows = query_piece.shape[1]
    key_sub_rows = math.gcd(piece_rows, 128)

    def key_inner_step(block_turn, state_now):
        key_acc, value_acc = state_now
        offset = block_turn * key_sub_rows
        query_part = lax.dynamic_slice_in_dim(query_piece, offset, key_sub_rows, 1)
        grad_part = lax.dynamic_slice_in_dim(grad_piece, offset, key_sub_rows, 1)
        lse_part = lax.dynamic_slice_in_dim(lse_whole, offset, key_sub_rows, 1)
        delta_part = lax.dynamic_slice_in_dim(delta_whole, offset, key_sub_rows, 1)
        far_pos, far_doc = block_places(offset, key_sub_rows)
        shares = probabilities(
            query_part, key_rows, far_pos, far_doc, query_pos, query_doc, lse_part
        )
        value_acc = value_acc + jnp.einsum(
            "bhqk,bqhd->bkhd",
            shares.astype(jnp.bfloat16),
            split_heads(grad_part),
            preferred_element_type=jnp.float32,
        )
        grad_scores = score_grads(shares, grad_part, value_rows, delta_part)
        key_acc = key_acc + score_scale * jnp.einsum(
            "bhqk,bqhd->bkhd",
            grad_scores,
            split_heads(query_part),
            preferred_element_type=jnp.float32,
        )
        return (key_acc, value_acc)

    grad_keys, grad_values = lax.fori_loop(
        0, piece_rows // key_sub_rows, key_inner_step, (head_zeros, head_zeros)
    )
    grad_mixed = jnp.concatenate(
        [
            grad_queries.reshape(total_rows, model_width),
            grad_keys.reshape(total_rows, model_width),
            grad_values.reshape(total_rows, model_width),
        ],
        axis=1,
    ).astype(jnp.bfloat16)
    qkv_grad = lax.psum_scatter(
        dot_cols(grad_mixed, hidden_one_low), ("batch", "ctx"), scatter_dimension=0, tiled=True
    )
    grad_hidden_one = jnp.dot(grad_mixed, qkv_back, preferred_element_type=jnp.float32)
    unused, pull_one = jax.vjp(norm_layer, tokens, vector_rows[0], vector_rows[1])
    grad_tokens_norm, grad_gain_one, grad_bias_one = pull_one(grad_hidden_one)
    input_grad = (
        (grad_middle + grad_tokens_norm).astype(jnp.bfloat16).reshape(groups, rows_seq, model_width)
    )
    mixed_sums = jnp.sum(grad_mixed.astype(jnp.float32), axis=0)
    fc_sums = jnp.sum(grad_before.astype(jnp.float32), axis=0)
    vector_local = jnp.concatenate(
        [
            jnp.stack(
                [
                    grad_gain_one,
                    grad_bias_one,
                    mixed_sums[:model_width],
                    mixed_sums[2 * model_width :],
                    jnp.sum(grad_middle, axis=0),
                    grad_gain_two,
                    grad_bias_two,
                    jnp.sum(grad_top_f, axis=0),
                ]
            ),
            fc_sums.reshape(-1, model_width),
        ],
        axis=0,
    )
    out_grad, vectors_grad = (
        lax.psum_scatter(out_term, ("batch", "ctx"), scatter_dimension=0, tiled=True),
        lax.psum_scatter(vector_local, ("batch", "ctx"), scatter_dimension=1, tiled=True),
    )
    qkv_moment_new, qkv_square_new, qkv_weight_new = adam_update(
        qkv_weight, qkv_moment, qkv_square, qkv_grad, rate_matrix, decay_matrix
    )
    out_moment_new, out_square_new, out_weight_new = adam_update(
        out_weight, out_moment, out_square, out_grad, rate_matrix, decay_matrix
    )
    fc_moment_new, fc_square_new, fc_weight_new = adam_update(
        fc_weight, fc_moment, fc_square, fc_grad, rate_matrix, decay_matrix
    )
    proj_moment_new, proj_square_new, proj_weight_new = adam_update(
        proj_weight, proj_moment, proj_square, proj_grad, rate_matrix, decay_matrix
    )
    vectors_moment_new, vectors_square_new, vectors_new = adam_update(
        vectors, vectors_moment, vectors_square, vectors_grad, rate_vector, 0.0
    )
    return (
        layer_out,
        input_grad,
        qkv_grad,
        qkv_moment_new,
        qkv_square_new,
        qkv_weight_new,
        out_grad,
        out_moment_new,
        out_square_new,
        out_weight_new,
        fc_grad,
        fc_moment_new,
        fc_square_new,
        fc_weight_new,
        proj_grad,
        proj_moment_new,
        proj_square_new,
        proj_weight_new,
        vectors_grad,
        vectors_moment_new,
        vectors_square_new,
        vectors_new,
    )


def solution(mesh):
    in_specs = (
        P("batch", "ctx", None),
        P("batch", "ctx", None),
        P("batch", None),
        P(("batch", "ctx"), None),
        P(("batch", "ctx"), None),
        P(("batch", "ctx"), None),
        P(("batch", "ctx"), None),
        P(("batch", "ctx"), None),
        P(("batch", "ctx"), None),
        P(("batch", "ctx"), None),
        P(("batch", "ctx"), None),
        P(("batch", "ctx"), None),
        P(("batch", "ctx"), None),
        P(("batch", "ctx"), None),
        P(("batch", "ctx"), None),
        P(None, ("batch", "ctx")),
        P(None, ("batch", "ctx")),
        P(None, ("batch", "ctx")),
    )
    out_specs = (
        P("batch", "ctx", None),
        P("batch", "ctx", None),
        P(("batch", "ctx"), None),
        P(("batch", "ctx"), None),
        P(("batch", "ctx"), None),
        P(("batch", "ctx"), None),
        P(("batch", "ctx"), None),
        P(("batch", "ctx"), None),
        P(("batch", "ctx"), None),
        P(("batch", "ctx"), None),
        P(("batch", "ctx"), None),
        P(("batch", "ctx"), None),
        P(("batch", "ctx"), None),
        P(("batch", "ctx"), None),
        P(("batch", "ctx"), None),
        P(("batch", "ctx"), None),
        P(("batch", "ctx"), None),
        P(("batch", "ctx"), None),
        P(None, ("batch", "ctx")),
        P(None, ("batch", "ctx")),
        P(None, ("batch", "ctx")),
        P(None, ("batch", "ctx")),
    )
    return jax.shard_map(local, mesh=mesh, in_specs=in_specs, out_specs=out_specs, check_vma=False)
```

profile of v0, /device:TPU:0, one launch (start us, length us, event | category | flops | bytes accessed | tf_op | source)
XLA Modules:
  0.0 950.0 jit_solution(11472819125550084990)
XLA Ops:
  9.6 43.9 %all-gather = bf16[32,24,12]{1,2,0:T(8,128)(2,1)S(1)} all-gather(bf16[1,24,12]{1,2,0:T(8,128)(2,1)S(1)} %convert_bitcast_fusion), channel_id=1, replica_groups=mesh['batch'=4,'ctx'=8] {'batch','ctx'}, dimensions={0}, use_global_device_ids=true | all-gather | bytes 19008 | tf_op jit(solution)/shard_map/all_gather | solution.py:145
  58.3 16.4 %all-gather.10.cloned.1.call-done = bf16[2304,768]{1,0:T(8,128)(2,1)} async-done(((bf16[72,768]{1,0:T(8,128)(2,1)}), bf16[2304,768]{1,0:T(8,128)(2,1)}) %all-gather.10.cloned.1.call-update) | async-done | bytes 3538960 | tf_op jit(solution)/shard_map/all_gather | solution.py:143
  74.7 3.1 fusion.61
  82.3 35.0 %all-gather.12.cloned.1.call-done = bf16[2,1024,768]{1,2,0:T(8,128)(2,1)} async-done(((bf16[2,128,768]{1,2,0:T(8,128)(2,1)}), bf16[2,1024,768]{1,2,0:T(8,128)(2,1)}) %all-gather.12.cloned.1.call-update) | async-done | bytes 3145744 | tf_op jit(solution)/shard_map/all_gather | solution.py:162
  117.3 39.0 %all-gather.14.cloned.1.call-done = bf16[2,1024,768]{1,2,0:T(8,128)(2,1)} async-done(((bf16[2,128,768]{1,2,0:T(8,128)(2,1)}), bf16[2,1024,768]{1,2,0:T(8,128)(2,1)}) %all-gather.14.cloned.1.call-update) | async-done | bytes 3145744 | tf_op jit(solution)/shard_map/all_gather | solution.py:163
  156.4 22.1 %while.60 = (s32[]{:T(128)}, f32[2,12,128,64]{2,3,1,0:T(8,128)S(1)}, f32[2,12,128]{2,1,0:T(8,128)S(1)}, f32[2,12,128]{2,1,0:T(8,128)S(1)}, s32[2,4]{0,1:T(4,128)...) while((s32[]{:T(128)}, ...), condition=%wide.wide.region_8.9_spmd.clone, body=%wide.wide.region_4.8_spmd.clone.sunk | while | flops 104900608 | bytes 9410291 | solution.py:186
  178.6 1.7 bitcast_convert_fusion
  180.3 31.9 %all-gather.16.cloned.1.call-done = bf16[768,768]{1,0:T(8,128)(2,1)} async-done(((bf16[24,768]{1,0:T(8,128)(2,1)}), bf16[768,768]{1,0:T(8,128)(2,1)}) %all-gather.16.cloned.1.call-update) | async-done | bytes 1179664 | tf_op jit(solution)/shard_map/all_gather | solution.py:144
  212.3 2.0 fusion.105
  214.5 63.8 %all-gather.18.cloned.1.call-done = bf16[3072,768]{1,0:T(8,128)(2,1)} async-done(((bf16[96,768]{1,0:T(8,128)(2,1)}), bf16[3072,768]{1,0:T(8,128)(2,1)}) %all-gather.18.cloned.1.call-update) | async-done | bytes 4718608 | tf_op jit(solution)/shard_map/all_gather | solution.py:201
  278.3 3.8 convolution_add_fusion.2
  282.2 1.6 copy-done.7
  283.9 5.8 fusion.92
  289.8 134.2 %reduce-scatter.12.cloned.1.call-done = f32[96,768]{1,0:T(8,128)} async-done(((f32[3072,768]{1,0:T(8,128)}), f32[96,768]{1,0:T(8,128)}) %reduce-scatter.12.cloned.1.call-update) | async-done | bytes 294928 | tf_op jit(solution)/shard_map/reduce_scatter | solution.py:218
  424.0 2.1 multiply_subtract_fusion
  427.4 63.6 %all-gather.20.cloned.1.call-done = bf16[3072,768]{1,0:T(8,128)(2,1)} async-done(((bf16[96,768]{1,0:T(8,128)(2,1)}), bf16[3072,768]{1,0:T(8,128)(2,1)}) %all-gather.20.cloned.1.call-update) | async-done | bytes 4718608 | tf_op jit(solution)/shard_map/all_gather | solution.py:208
  491.0 7.3 convert_reduce_fusion
  498.4 5.3 multiply_reduce_fusion
  509.3 15.7 %all_gather.47 = f32[2,1024,12]{1,2,0:T(8,128)} all-gather(f32[2,128,12]{1,2,0:T(8,128)S(1)} %bitcast.281), channel_id=1, replica_groups=mesh['batch'=4,'ctx'=8] {'ctx'}, dimensions={1}, use_global_device_ids=true | all-gather | bytes 110592 | tf_op jit(solution)/shard_map/all_gather | solution.py:251
  531.4 1.9 reshape_reshape.63
  533.2 2.9 fusion.73
  536.2 52.7 %while.61 = (s32[]{:T(128)}, f32[2,128,12,64]{1,3,2,0:T(8,128)}, bf16[2,1024,768]{1,2,0:T(8,128)(2,1)}, s32[2,4]{0,1:T(4,128)S(1)}, s32[2,128]{1,0:T(2,128)S(1)}...) while((s32[]{:T(128)}, f32[2,128,12,64]{1,3,2,0:T(8,128)}, ...), condition=%wide.wide.region_16.17_spmd.clone, body=%wide.wide.region_14.16_spmd.clone.sunk | while | flops 154430464 | bytes 8386305 | solution.py:273
  536.2 1.9 constant_dynamic-slice_fusion.18
  539.5 3.1 fusion.204
  542.6 1.9 constant_dynamic-slice_fusion.18
  545.9 3.3 fusion.204
  549.2 1.9 constant_dynamic-slice_fusion.18
  552.5 3.4 fusion.204
  555.9 1.9 constant_dynamic-slice_fusion.18
  559.1 3.4 fusion.204
  562.5 1.9 constant_dynamic-slice_fusion.18
  565.8 3.3 fusion.204
  569.1 1.9 constant_dynamic-slice_fusion.18
  572.4 3.3 fusion.204
  575.7 1.9 constant_dynamic-slice_fusion.18
  579.0 3.3 fusion.204
  582.3 1.9 constant_dynamic-slice_fusion.18
  585.6 3.4 fusion.204
  590.7 11.7 %all_gather.49 = f32[2,1024,12]{1,0,2:T(2,128)} all-gather(f32[2,128,12]{1,0,2:T(2,128)} %copy-done.42), channel_id=1, replica_groups=mesh['batch'=4,'ctx'=8] {'ctx'}, dimensions={1}, use_global_device_ids=true | all-gather | bytes 110592 | tf_op jit(solution)/shard_map/all_gather | solution.py:252
  603.3 5.8 fusion.91
  609.5 63.9 %while.62 = (s32[]{:T(128)}, f32[2,128,12,64]{1,3,2,0:T(8,128)S(1)}, f32[2,128,12,64]{1,3,2,0:T(8,128)}, bf16[2,1024,768]{1,2,0:T(8,128)(2,1)}, s32[2,128]{1,0:T...) while((s32[]{:T(128)}, ...), condition=%wide.wide.region_19.20_spmd.clone, body=%wide.wide.region_17.19_spmd.clone.sunk | while | flops 205548544 | bytes 12007554 | solution.py:305
  611.7 1.7 exponential_select_fusion.4
  618.7 1.7 exponential_select_fusion.4
  622.2 2.4 fusion.215
  626.8 1.7 exponential_select_fusion.4
  630.3 2.4 fusion.215
  635.0 1.7 exponential_select_fusion.4
  638.5 2.4 fusion.215
  643.1 1.8 exponential_select_fusion.4
  646.6 2.4 fusion.215
  651.2 1.7 exponential_select_fusion.4
  654.7 2.4 fusion.215
  659.4 1.7 exponential_select_fusion.4
  662.9 2.4 fusion.215
  667.5 1.7 exponential_select_fusion.4
  671.0 2.4 fusion.215
  675.6 4.0 fusion.106
  681.0 6.0 fusion.71
  688.7 3.4 fusion.93
  693.2 39.9 %all-reduce = f32[12,768]{1,0:T(8,128)S(1)} all-reduce(f32[12,768]{1,0:T(8,128)S(1)} %concatenate.12), channel_id=6, replica_groups=mesh['batch'=4,'ctx'=8] {'batch','ctx'}, use_global_device_ids=true, to_apply=%region_34.35.clone | all-reduce | flops 9216 | bytes 73728
  734.8 81.1 %reduce-scatter.10.cloned.1.call-done = f32[96,768]{1,0:T(8,128)} async-done(((f32[3072,768]{1,0:T(8,128)}), f32[96,768]{1,0:T(8,128)}) %reduce-scatter.10.cloned.1.call-update) | async-done | bytes 294928 | tf_op jit(solution)/shard_map/reduce_scatter | solution.py:225
  816.0 2.2 multiply_subtract_fusion.1
  818.2 122.8 %reduce-scatter.6.cloned.1.call-done = f32[72,768]{1,0:T(8,128)} async-done(((f32[2304,768]{1,0:T(8,128)}), f32[72,768]{1,0:T(8,128)}) %reduce-scatter.6.cloned.1.call-update) | async-done | bytes 221200 | tf_op jit(solution)/shard_map/reduce_scatter | solution.py:316
  941.0 2.2 multiply_subtract_fusion.2
  (503 shorter events, 100.0 us)
Async XLA Ops:
  7.2 67.5 %all-gather.10.cloned.1.call-start = ((), (), s32[]{:S(2)}) async-start(), calls=%async_computation.4 | async-start | bytes 3649536 | tf_op jit(solution)/shard_map/all_gather | solution.py:143
  8.9 108.5 %all-gather.12.cloned.1.call-start = ((), (), s32[]{:S(2)}) async-start(), calls=%async_computation.5 | async-start | bytes 3538944 | tf_op jit(solution)/shard_map/all_gather | solution.py:162
  54.6 20.2 %copy-start.45 = (f32[768]{0:T(1024)}, f32[768]{0:T(1024)S(1)}, u32[]{:S(2)}) copy-start(f32[768]{0:T(1024)S(1)} %get-tuple-element.1228) | copy-start | bytes 9220
  54.6 223.7 %copy-start.57 = (f32[768]{0:T(1024)}, f32[768]{0:T(1024)S(1)}, u32[]{:S(2)}) copy-start(f32[768]{0:T(1024)S(1)} %get-tuple-element.1223) | copy-start | bytes 9220
  54.6 449.1 %copy-start.48 = (f32[768]{0:T(1024)}, f32[768]{0:T(1024)S(1)}, u32[]{:S(2)}) copy-start(f32[768]{0:T(1024)S(1)} %get-tuple-element.1221) | copy-start | bytes 9220
  55.7 22.1 %copy-start.51 = (f32[256]{0:T(256)}, f32[256]{0:T(256)S(1)}, u32[]{:S(2)}) copy-start(f32[256]{0:T(256)S(1)} %get-tuple-element.1341) | copy-start | bytes 3076
  57.0 17.7 %copy-start.61 = (f32[2,128]{1,0:T(2,128)}, f32[2,128]{1,0:T(2,128)S(1)}, u32[]{:S(2)}) copy-start(f32[2,128]{1,0:T(2,128)S(1)} %multiply_reduce_fusion.5) | copy-start | bytes 3076
  57.0 20.9 %copy-start.53 = (f32[256]{0:T(256)}, f32[256]{0:T(256)S(1)}, u32[]{:S(2)}) copy-start(f32[256]{0:T(256)S(1)} %bitcast_rsqrt_fusion) | copy-start | bytes 3076
  58.3 16.4 %copy-start.20 = (bf16[256,768]{1,0:T(8,128)(2,1)}, bf16[256,768]{1,0:T(8,128)(2,1)S(1)}, u32[]{:S(2)}) copy-start(bf16[256,768]{1,0:T(8,128)(2,1)S(1)} %add_convert_fusion.2) | copy-start | bytes 1179652
  78.0 4.0 copy-start.12
  79.2 77.2 %all-gather.14.cloned.1.call-start = ((), (), s32[]{:S(2)}) async-start(), calls=%async_computation.6 | async-start | bytes 3538944 | tf_op jit(solution)/shard_map/all_gather | solution.py:163
  80.2 132.1 %all-gather.16.cloned.1.call-start = ((), (), s32[]{:S(2)}) async-start(), calls=%async_computation.7 | async-start | bytes 1216512 | tf_op jit(solution)/shard_map/all_gather | solution.py:144
  80.9 197.4 %all-gather.18.cloned.1.call-start = ((), (), s32[]{:S(2)}) async-start(), calls=%async_computation.8 | async-start | bytes 4866048 | tf_op jit(solution)/shard_map/all_gather | solution.py:201
  81.7 342.4 %reduce-scatter.12.cloned.1.call-start = ((), (), s32[]{:S(2)}) async-start(), calls=%async_computation.15 | async-start | bytes 9732096 | tf_op jit(solution)/shard_map/reduce_scatter | solution.py:218
  82.2 74.2 %copy-start.14 = (bf16[256,768]{0,1:T(8,128)(2,1)}, bf16[256,768]{0,1:T(8,128)(2,1)S(1)}, u32[]{:S(2)}) copy-start(bf16[256,768]{0,1:T(8,128)(2,1)S(1)} %copy.130) | copy-start | bytes 1179652
  178.5 103.7 %copy-start.28 = (f32[2,12,128]{2,1,0:T(8,128)}, f32[2,12,128]{2,1,0:T(8,128)S(1)}, u32[]{:S(2)}) copy-start(f32[2,12,128]{2,1,0:T(8,128)S(1)} %get-tuple-element.950) | copy-start | bytes 36868
  178.5 103.7 %copy-start.29 = (s32[2,4]{0,1:T(4,128)}, s32[2,4]{0,1:T(4,128)S(1)}, u32[]{:S(2)}) copy-start(s32[2,4]{0,1:T(4,128)S(1)} %get-tuple-element.1942) | copy-start | bytes 100
  178.5 103.7 %copy-start.38 = (s32[2,128]{1,0:T(2,128)}, s32[2,128]{1,0:T(2,128)S(1)}, u32[]{:S(2)}) copy-start(s32[2,128]{1,0:T(2,128)S(1)} %get-tuple-element.1952) | copy-start | bytes 3076
  180.3 101.9 %copy-start.24 = (bf16[2,128,12,64]{1,0,3,2:T(2,128)(2,1)}, bf16[2,128,12,64]{1,0,3,2:T(2,128)(2,1)S(1)}, u32[]{:S(2)}) copy-start(bf16[2,128,12,64]{1,0,3,2:T(2,128)(2,1)S(1)} %get-tuple-element.1319) | copy-start | bytes 1179652
  214.2 289.4 %copy-start.4 = (f32[256,768]{1,0:T(8,128)}, f32[256,768]{1,0:T(8,128)S(1)}, u32[]{:S(2)}) copy-start(f32[256,768]{1,0:T(8,128)S(1)} %get-tuple-element.1344) | copy-start | bytes 2359300
  214.2 289.4 %copy-start.55 = (f32[256]{0:T(256)}, f32[256]{0:T(256)S(1)}, u32[]{:S(2)}) copy-start(f32[256]{0:T(256)S(1)} %broadcast_multiply_fusion) | copy-start | bytes 3076
  214.5 289.2 %copy-start.60 = (f32[256]{0:T(256)}, f32[256]{0:T(256)S(1)}, u32[]{:S(2)}) copy-start(f32[256]{0:T(256)S(1)} %fusion.86) | copy-start | bytes 3076
  278.3 5.5 copy-start.16
  289.7 134.3 %copy-start.33 = (f32[96,768]{1,0:T(8,128)S(1)}, f32[96,768]{1,0:T(8,128)}, u32[]{:S(2)}) copy-start(f32[96,768]{1,0:T(8,128)} %param.36) | copy-start | bytes 884740
  289.7 134.3 %copy-start.34 = (f32[96,768]{1,0:T(8,128)S(1)}, f32[96,768]{1,0:T(8,128)}, u32[]{:S(2)}) copy-start(f32[96,768]{1,0:T(8,128)} %param.38) | copy-start | bytes 884740
  289.7 134.3 %copy-start.35 = (f32[96,768]{1,0:T(8,128)S(1)}, f32[96,768]{1,0:T(8,128)}, u32[]{:S(2)}) copy-start(f32[96,768]{1,0:T(8,128)} %param.37) | copy-start | bytes 884740
  289.7 136.5 %copy-start.13 = (bf16[256,768]{1,0:T(8,128)(2,1)S(1)}, bf16[256,768]{1,0:T(8,128)(2,1)}, u32[]{:S(2)}) copy-start(bf16[256,768]{1,0:T(8,128)(2,1)} %copy-done.12) | copy-start | bytes 1179652
  289.8 201.3 %all-gather.20.cloned.1.call-start = ((), (), s32[]{:S(2)}) async-start(), calls=%async_computation.9 | async-start | bytes 4866048 | tf_op jit(solution)/shard_map/all_gather | solution.py:208
  426.1 183.3 %all-gather.22.cloned.1.call-start = ((), (), s32[]{:S(2)}) async-start(), calls=%async_computation.10 | async-start | bytes 3538944 | tf_op jit(solution)/shard_map/all_gather | solution.py:274
  427.1 182.3 %all-gather.24.cloned.1.call-start = ((), (), s32[]{:S(2)}) async-start(), calls=%async_computation.11 | async-start | bytes 3538944 | tf_op jit(solution)/shard_map/all_gather | solution.py:275
  498.4 5.3 copy-start.18
  504.8 28.4 %copy-start = (f32[256,768]{1,0:T(8,128)}, f32[256,768]{1,0:T(8,128)S(1)}, u32[]{:S(2)}) copy-start(f32[256,768]{1,0:T(8,128)S(1)} %get-tuple-element.1304) | copy-start | bytes 2359300
  506.4 180.6 %reduce-scatter.8.cloned.1.call-start = ((), (), s32[]{:S(2)}) async-start(), calls=%async_computation.13 | async-start | bytes 2433024 | tf_op jit(solution)/shard_map/reduce_scatter | solution.py:346
  506.8 23.3 %copy-start.22 = (bf16[256,768]{0,1:T(8,128)(2,1)}, bf16[256,768]{0,1:T(8,128)(2,1)S(1)}, u32[]{:S(2)}) copy-start(bf16[256,768]{0,1:T(8,128)(2,1)S(1)} %copy.140) | copy-start | bytes 1179652
  507.0 19.0 %copy-start.23 = (bf16[256,768]{0,1:T(8,128)(2,1)}, bf16[256,768]{0,1:T(8,128)(2,1)S(1)}, u32[]{:S(2)}) copy-start(bf16[256,768]{0,1:T(8,128)(2,1)S(1)} %copy.141) | copy-start | bytes 1179652
  536.1 279.8 %reduce-scatter.10.cloned.1.call-start = ((), (), s32[]{:S(2)}) async-start(), calls=%async_computation.14 | async-start | bytes 9732096 | tf_op jit(solution)/shard_map/reduce_scatter | solution.py:225
  536.2 67.0 %copy-start.49 = (f32[768]{0:T(1024)S(1)}, f32[768]{0:T(1024)}, u32[]{:S(2)}) copy-start(f32[768]{0:T(1024)} %copy-done.48) | copy-start | bytes 9220
  536.2 67.0 %copy-start.56 = (f32[256]{0:T(256)S(1)}, f32[256]{0:T(256)}, u32[]{:S(2)}) copy-start(f32[256]{0:T(256)} %copy-done.55) | copy-start | bytes 3076
  589.0 14.3 %copy-start.5 = (f32[256,768]{1,0:T(8,128)S(1)}, f32[256,768]{1,0:T(8,128)}, u32[]{:S(2)}) copy-start(f32[256,768]{1,0:T(8,128)} %copy-done.4) | copy-start | bytes 2359300
  589.0 14.3 %copy-start.19 = (bf16[256,3072]{1,0:T(8,128)(2,1)S(1)}, bf16[256,3072]{1,0:T(8,128)(2,1)}, u32[]{:S(2)}) copy-start(bf16[256,3072]{1,0:T(8,128)(2,1)} %copy-done.18) | copy-start | bytes 4718596
  609.1 331.8 %reduce-scatter.6.cloned.1.call-start = ((), (), s32[]{:S(2)}) async-start(), calls=%async_computation.12 | async-start | bytes 7299072 | tf_op jit(solution)/shard_map/reduce_scatter | solution.py:316
  609.5 4.0 copy-start.31
  609.5 4.0 copy-start.40
  616.5 4.0 copy-start.40
  624.6 4.0 copy-start.40
  632.7 4.0 copy-start.31
  632.7 4.0 copy-start.40
  640.9 4.0 copy-start.31
  640.9 4.0 copy-start.40
  649.0 4.0 copy-start.31
  649.0 4.0 copy-start.40
  657.1 4.0 copy-start.40
  665.2 4.0 copy-start.40
  681.0 6.1 copy-start.37
  681.0 6.1 copy-start.43
  681.0 6.1 copy-start.44
  681.0 7.7 copy-start.2
  681.0 7.7 copy-start.46
  681.0 7.7 copy-start.52
  688.7 44.3 %copy-start.50 = (f32[12,24]{1,0:T(8,128)S(1)}, f32[12,24]{1,0:T(8,128)}, u32[]{:S(2)}) copy-start(f32[12,24]{1,0:T(8,128)} %param.39) | copy-start | bytes 3460
  688.7 44.3 %copy-start.63 = (f32[12,24]{1,0:T(8,128)S(1)}, f32[12,24]{1,0:T(8,128)}, u32[]{:S(2)}) copy-start(f32[12,24]{1,0:T(8,128)} %param.41) | copy-start | bytes 3460
  688.7 44.3 %copy-start.64 = (f32[12,24]{1,0:T(8,128)S(1)}, f32[12,24]{1,0:T(8,128)}, u32[]{:S(2)}) copy-start(f32[12,24]{1,0:T(8,128)} %param.40) | copy-start | bytes 3460
  692.2 41.6 %copy-start.1 = (f32[256,768]{1,0:T(8,128)S(1)}, f32[256,768]{1,0:T(8,128)}, u32[]{:S(2)}) copy-start(f32[256,768]{1,0:T(8,128)} %copy-done) | copy-start | bytes 2359300
  692.2 123.8 %copy-start.27 = (f32[96,768]{1,0:T(8,128)S(1)}, f32[96,768]{1,0:T(8,128)}, u32[]{:S(2)}) copy-start(f32[96,768]{1,0:T(8,128)} %param.33) | copy-start | bytes 884740
  (45 other events, 105.8 us)
Sparse Core Ops, SparseCore 0:
  11.6 63.0 all-gather.9
  79.3 37.9 all-gather.11
  118.9 37.4 all-gather.13
  159.8 52.4 all-gather.15
  215.7 62.5 all-gather.17
  289.9 134.1 reduce-scatter.11
  428.1 62.8 all-gather.19
  492.7 39.0 all-gather.21
  533.4 37.4 all-gather.23
  577.5 97.2 reduce-scatter.7
  681.3 134.6 reduce-scatter.9
  823.0 117.8 reduce-scatter.5
where the time goes:
time: 953 us; the launch traced here: 950 us
  waiting for transfers between devices  588 us (62%)
  matrix products  127 us (13%)
  blocking collectives  111 us (12%)
  local copies, waits for them, and re-layouts  65.5 us (7%)
  other arithmetic  40.5 us (4%)
  between operations  15.3 us (2%)
    reduce_scatter x1, waiting for transfers between devices, local(): lax.psum_scatter(dot_cols(active_low, grad_top), ('batch', 'ctx'), scatte...  134 us
    reduce_scatter x1, waiting for transfers between devices, local(): lax.psum_scatter(dot_cols(grad_mixed, hidden_one_low), ('batch', 'ctx'),...  123 us
    reduce_scatter x1, waiting for transfers between devices, local(): lax.psum_scatter(dot_cols(grad_before, hidden_two_low), ('batch', 'ctx'),...  81.1 us
    all_gather x1, waiting for transfers between devices, local(): pieces = lax.all_gather(fc_low, ('batch', 'ctx'), axis=0, tiled=True)  63.8 us
    all_gather x1, waiting for transfers between devices, local(): lax.all_gather(proj_low, ('batch', 'ctx'), axis=0, tiled=True)  63.6 us
    all_gather x1, blocking collectives, local(): lax.all_gather(vectors.astype(jnp.bfloat16), ('batch', 'ctx'), axis=1, ti...  43.9 us
    unnamed x1, blocking collectives  39.9 us
    all_gather x1, waiting for transfers between devices, local(): value_piece = lax.all_gather(value_rows, 'ctx', axis=1, tiled=True)  39 us
  transfers between devices with their start and end apart: 12, of which 9 were waited for; matrix products, arithmetic and copies ran while one was open for 22% of the time, Pallas kernels for 0%

commit v1 on v0

v1 whole, which is shorter than its diff:
```python
import functools

import jax
import jax.numpy as jnp
from jax import lax
from jax.experimental import pallas as pl
from jax.experimental.pallas import tpu as pltpu
from jax.sharding import PartitionSpec as P

H = 12
HD = 64
STEP = 10


norm_eps = 1e-05
beta_one = 0.9
beta_two = 0.95
adam_eps = 1e-08
rate_matrix = 0.1
rate_vector = 0.6
decay_matrix = 0.1
score_scale = 0.125
masked_score = -1e30


def norm_layer(values, norm_gain, norm_bias):
    center = values - jnp.mean(values, axis=-1, keepdims=True)
    spread = jnp.mean(center * center, axis=-1, keepdims=True)
    return center * lax.rsqrt(spread + norm_eps) * norm_gain + norm_bias


def gelu_tanh(values):
    return jax.nn.gelu(values, approximate=True)


def natural_positions(row_index, seq_rows, ctx_count):
    device = row_index // seq_rows
    within = row_index % seq_rows
    half_rows = seq_rows // 2
    block_id = jnp.where(within < half_rows, device, 2 * ctx_count - 1 - device)
    return block_id * half_rows + within % half_rows


def dot_rows(left, right):
    return lax.dot_general(
        left, right, (((1,), (1,)), ((), ())), preferred_element_type=jnp.float32
    )


def dot_cols(left, right):
    return lax.dot_general(
        left, right, (((0,), (0,)), ((), ())), preferred_element_type=jnp.float32
    )


def adam_update(weight, moment, square, gradient, rate, decay):
    moment_new = beta_one * moment + (1.0 - beta_one) * gradient
    square_new = beta_two * square + (1.0 - beta_two) * gradient * gradient
    corrected = moment_new / (1.0 - beta_one**STEP)
    scaled = square_new / (1.0 - beta_two**STEP)
    weight_new = weight - rate * (corrected / (jnp.sqrt(scaled) + adam_eps) + decay * weight)
    return (moment_new, square_new, weight_new)


def attention_forward_kernel(pairs, query_ref, whole_ref, low_ref, qpos_ref, kpos_ref, out_ref, exact_ref, lse_ref):
    width = pairs * HD
    key_pos = kpos_ref[...]
    query_pos = qpos_ref[...]
    causal = key_pos <= query_pos
    for pair in range(pairs):
        lanes = slice(pair * HD, (pair + 1) * HD)
        queries = query_ref[:, pair * HD : (pair + 1) * HD]
        keys = whole_ref[:, width + pair * HD : width + (pair + 1) * HD]
        values = whole_ref[:, 2 * width + pair * HD : 2 * width + (pair + 1) * HD]
        allowed = causal & (key_pos >= low_ref[:, pair : pair + 1])
        scores = jnp.where(allowed, dot_rows(queries, keys) * score_scale, masked_score)
        top = jnp.max(scores, axis=1, keepdims=True)
        weights = jnp.exp(scores - top)
        total = jnp.sum(weights, axis=1, keepdims=True)
        shares = (weights * (1.0 / total)).astype(jnp.bfloat16)
        attended = jnp.dot(shares, values, preferred_element_type=jnp.float32)
        exact_ref[:, lanes] = attended
        out_ref[:, lanes] = attended.astype(jnp.bfloat16)
        lse_ref[:, pair : pair + 1] = top + jnp.log(total)


def attention_backward_kernel(
    pairs, steps, query_ref, whole_ref, low_ref, qpos_ref, kpos_ref, exact_ref, lse_ref, grad_ref,
    out_ref, key_acc, value_acc,
):
    width = pairs * HD
    step = pl.program_id(0)
    rows = query_ref.shape[0]
    key_pos = kpos_ref[...]
    query_pos = qpos_ref[...]
    causal = key_pos <= query_pos

    @pl.when(step == 0)
    def _():
        key_acc[...] = jnp.zeros_like(key_acc)
        value_acc[...] = jnp.zeros_like(value_acc)

    here = pl.ds(pl.multiple_of(step * rows, rows), rows)
    for pair in range(pairs):
        lanes = slice(pair * HD, (pair + 1) * HD)
        queries = query_ref[:, lanes]
        keys = whole_ref[:, width + pair * HD : width + (pair + 1) * HD]
        values = whole_ref[:, 2 * width + pair * HD : 2 * width + (pair + 1) * HD]
        grads = grad_ref[:, lanes]
        allowed = causal & (key_pos >= low_ref[:, pair : pair + 1])
        scores = dot_rows(queries, keys) * score_scale
        shares = jnp.where(allowed, jnp.exp(scores - lse_ref[:, pair : pair + 1]), 0.0)
        delta = jnp.sum(grads.astype(jnp.float32) * exact_ref[:, lanes], axis=1, keepdims=True)
        grad_scores = (shares * (dot_rows(grads, values) - delta)).astype(jnp.bfloat16)
        out_ref[here, lanes] = (
            score_scale * jnp.dot(grad_scores, keys, preferred_element_type=jnp.float32)
        ).astype(jnp.bfloat16)
        key_acc[:, lanes] += dot_cols(grad_scores, queries)
        value_acc[:, lanes] += dot_cols(shares.astype(jnp.bfloat16), grads)

    @pl.when(step == steps - 1)
    def _():
        out_ref[:, width : 2 * width] = (score_scale * key_acc[...]).astype(jnp.bfloat16)
        out_ref[:, 2 * width :] = value_acc[...].astype(jnp.bfloat16)


def query_block(length):
    return 256 if length <= 1024 else 64


def attention_specs(length, pairs, block):
    return [
        pl.BlockSpec((block, 3 * pairs * HD), lambda i: (i, 0)),
        pl.BlockSpec((length, 3 * pairs * HD), lambda i: (0, 0)),
        pl.BlockSpec((block, pairs), lambda i: (i, 0)),
        pl.BlockSpec((block, 1), lambda i: (i, 0)),
        pl.BlockSpec((1, length), lambda i: (0, 0)),
    ]


def attention_forward(mixed, low, qpos, kpos):
    length, pairs = low.shape
    block = query_block(length)
    width = pairs * HD
    return pl.pallas_call(
        functools.partial(attention_forward_kernel, pairs),
        grid=(length // block,),
        in_specs=attention_specs(length, pairs, block),
        out_specs=[
            pl.BlockSpec((block, width), lambda i: (i, 0)),
            pl.BlockSpec((block, width), lambda i: (i, 0)),
            pl.BlockSpec((block, pairs), lambda i: (i, 0)),
        ],
        out_shape=[
            jax.ShapeDtypeStruct((length, width), jnp.bfloat16),
            jax.ShapeDtypeStruct((length, width), jnp.float32),
            jax.ShapeDtypeStruct((length, pairs), jnp.float32),
        ],
        compiler_params=pltpu.CompilerParams(vmem_limit_bytes=48 * 2**20),
        name="attention_forward",
    )(mixed, mixed, low, qpos, kpos)


def attention_backward(mixed, low, qpos, kpos, exact, lse, grads):
    length, pairs = low.shape
    block = query_block(length)
    width = pairs * HD
    return pl.pallas_call(
        functools.partial(attention_backward_kernel, pairs, length // block),
        grid=(length // block,),
        in_specs=attention_specs(length, pairs, block)
        + [
            pl.BlockSpec((block, width), lambda i: (i, 0)),
            pl.BlockSpec((block, pairs), lambda i: (i, 0)),
            pl.BlockSpec((block, width), lambda i: (i, 0)),
        ],
        out_specs=pl.BlockSpec((length, 3 * width), lambda i: (0, 0)),
        out_shape=jax.ShapeDtypeStruct((length, 3 * width), jnp.bfloat16),
        scratch_shapes=[
            pltpu.VMEM((length, width), jnp.float32),
            pltpu.VMEM((length, width), jnp.float32),
        ],
        compiler_params=pltpu.CompilerParams(vmem_limit_bytes=48 * 2**20),
        name="attention_backward",
    )(mixed, mixed, low, qpos, kpos, exact, lse, grads)


def tokens_to_heads(array, parts, count, pairs):
    groups, rows, width = array.shape
    array = array.reshape(groups, rows, parts, H, HD).transpose(0, 3, 1, 2, 4)
    array = array.reshape(groups * H, rows, parts, HD)
    spare = count * pairs - groups * H
    if spare:
        array = jnp.pad(array, ((0, spare), (0, 0), (0, 0), (0, 0)))
    array = array.reshape(count, pairs, rows, parts, HD).transpose(0, 2, 3, 1, 4)
    array = array.reshape(count, rows, parts * pairs * HD)
    array = lax.all_to_all(array, "ctx", 0, 0)
    return array.reshape(count * rows, parts * pairs * HD)


def heads_to_tokens(array, parts, count, pairs, groups):
    rows = array.shape[0] // count
    array = lax.all_to_all(array.reshape(count, rows, parts * pairs * HD), "ctx", 0, 0)
    array = array.reshape(count, rows, parts, pairs, HD).transpose(0, 3, 1, 2, 4)
    array = array.reshape(count * pairs, rows, parts, HD)[: groups * H]
    array = array.reshape(groups, H, rows, parts, HD).transpose(0, 2, 3, 1, 4)
    return array.reshape(groups * rows, parts * H * HD)


def local(
    inputs,
    cotangent,
    lengths,
    qkv_weight,
    qkv_moment,
    qkv_square,
    out_weight,
    out_moment,
    out_square,
    fc_weight,
    fc_moment,
    fc_square,
    proj_weight,
    proj_moment,
    proj_square,
    vectors,
    vectors_moment,
    vectors_square,
):
    groups, rows_seq, model_width = inputs.shape
    total_rows = groups * rows_seq
    ctx_count = lax.axis_size("ctx")
    device_count = ctx_count * lax.axis_size("batch")
    both = ("batch", "ctx")
    length = rows_seq * ctx_count
    pairs = -(-(groups * H) // ctx_count)

    positions = natural_positions(jnp.arange(length, dtype=jnp.int32), rows_seq, ctx_count)
    ends = jnp.cumsum(lengths, axis=1)[:, :-1]
    starts = jnp.max(
        jnp.where(positions[None, :, None] >= ends[:, None, :], ends[:, None, :], 0), axis=2
    )
    pair_seq = jnp.minimum((lax.axis_index("ctx") * pairs + jnp.arange(pairs)) // H, groups - 1)
    chosen = (pair_seq[:, None] == jnp.arange(groups)[None, :]).astype(jnp.int32)
    low = jnp.sum(starts.T[:, None, :] * chosen[None, :, :], axis=2)
    qpos, kpos = positions[:, None], positions[None, :]

    qkv_rows, out_rows = qkv_weight.shape[0], out_weight.shape[0]
    vector_cols = vectors.shape[1]
    vector_entries = vectors.size
    weight_rows = qkv_rows + out_rows
    shard_rows = -(-(weight_rows + -(-vector_entries // model_width)) // 16) * 16
    vector_tail = (shard_rows - weight_rows) * model_width - vector_entries
    vector_line = jnp.pad(vectors.reshape(-1), (0, vector_tail)).reshape(-1, model_width)
    first_shard = jnp.concatenate([qkv_weight, out_weight, vector_line], axis=0).astype(jnp.bfloat16)
    first_full = lax.all_gather(first_shard, both, axis=0, tiled=False)
    fc_full = lax.all_gather(fc_weight.astype(jnp.bfloat16), both, axis=0, tiled=True)
    proj_full = lax.all_gather(proj_weight.astype(jnp.bfloat16), both, axis=0, tiled=True)
    qkv_full = first_full[:, :qkv_rows].reshape(-1, model_width)
    out_full = first_full[:, qkv_rows : qkv_rows + out_rows].reshape(-1, model_width)
    vector_rows = (
        first_full[:, qkv_rows + out_rows :]
        .reshape(device_count, -1)[:, :vector_entries]
        .reshape(device_count, vectors.shape[0], vector_cols)
        .transpose(1, 0, 2)
        .reshape(vectors.shape[0], model_width)
        .astype(jnp.float32)
    )
    tokens = inputs.reshape(total_rows, model_width).astype(jnp.float32)
    hidden_one_low = norm_layer(tokens, vector_rows[0], vector_rows[1]).astype(jnp.bfloat16)
    bias_qkv = jnp.concatenate(
        [vector_rows[2], jnp.zeros((model_width,), jnp.float32), vector_rows[3]]
    )
    mixed_low = (dot_rows(hidden_one_low, qkv_full) + bias_qkv).astype(jnp.bfloat16)
    mixed_heads = tokens_to_heads(
        mixed_low.reshape(groups, rows_seq, 3 * model_width), 3, ctx_count, pairs
    )
    attended_heads, exact_heads, lse = attention_forward(mixed_heads, low, qpos, kpos)
    attended_low = heads_to_tokens(attended_heads, 1, ctx_count, pairs, groups)
    middle = (
        tokens
        + jnp.dot(attended_low, out_full, preferred_element_type=jnp.float32)
        + vector_rows[4]
    )
    hidden_two_low = norm_layer(middle, vector_rows[5], vector_rows[6]).astype(jnp.bfloat16)
    bias_fc = vector_rows[8:].reshape(-1)
    before = dot_rows(hidden_two_low, fc_full) + bias_fc
    active_low = gelu_tanh(before).astype(jnp.bfloat16)
    mlp_out = jnp.dot(active_low, proj_full, preferred_element_type=jnp.float32)
    layer_out = (
        (middle + mlp_out + vector_rows[7])
        .astype(jnp.bfloat16)
        .reshape(groups, rows_seq, model_width)
    )
    grad_top = cotangent.reshape(total_rows, model_width)
    grad_top_f = grad_top.astype(jnp.float32)
    proj_grad = lax.psum_scatter(
        dot_cols(active_low, grad_top).astype(jnp.bfloat16), both, scatter_dimension=0, tiled=True
    ).astype(jnp.float32)
    grad_active = dot_rows(grad_top, proj_full)
    unused, pullback = jax.vjp(gelu_tanh, before)
    grad_before = pullback(grad_active)[0].astype(jnp.bfloat16)
    fc_grad = lax.psum_scatter(
        dot_cols(grad_before, hidden_two_low).astype(jnp.bfloat16),
        both,
        scatter_dimension=0,
        tiled=True,
    ).astype(jnp.float32)
    grad_hidden_two = jnp.dot(grad_before, fc_full, preferred_element_type=jnp.float32)
    unused, pull_two = jax.vjp(norm_layer, middle, vector_rows[5], vector_rows[6])
    grad_middle_norm, grad_gain_two, grad_bias_two = pull_two(grad_hidden_two)
    grad_middle = grad_top_f + grad_middle_norm
    grad_middle_low = grad_middle.astype(jnp.bfloat16)
    out_term = dot_cols(attended_low, grad_middle_low)
    grad_attended = dot_rows(grad_middle_low, out_full).astype(jnp.bfloat16)
    grad_heads = tokens_to_heads(
        grad_attended.reshape(groups, rows_seq, model_width), 1, ctx_count, pairs
    )
    mixed_grad_heads = attention_backward(
        mixed_heads, low, qpos, kpos, exact_heads, lse, grad_heads
    )
    grad_mixed = heads_to_tokens(mixed_grad_heads, 3, ctx_count, pairs, groups)
    qkv_term = dot_cols(grad_mixed, hidden_one_low)
    grad_hidden_one = jnp.dot(grad_mixed, qkv_full, preferred_element_type=jnp.float32)
    unused, pull_one = jax.vjp(norm_layer, tokens, vector_rows[0], vector_rows[1])
    grad_tokens_norm, grad_gain_one, grad_bias_one = pull_one(grad_hidden_one)
    input_grad = (
        (grad_middle + grad_tokens_norm).astype(jnp.bfloat16).reshape(groups, rows_seq, model_width)
    )
    mixed_sums = jnp.sum(grad_mixed.astype(jnp.float32), axis=0)
    fc_sums = jnp.sum(grad_before.astype(jnp.float32), axis=0)
    vector_local = jnp.concatenate(
        [
            jnp.stack(
                [
                    grad_gain_one,
                    grad_bias_one,
                    mixed_sums[:model_width],
                    mixed_sums[2 * model_width :],
                    jnp.sum(grad_middle, axis=0),
                    grad_gain_two,
                    grad_bias_two,
                    jnp.sum(grad_top_f, axis=0),
                ]
            ),
            fc_sums.reshape(-1, model_width),
        ],
        axis=0,
    )
    vector_term = jnp.pad(
        vector_local.reshape(-1, device_count, vector_cols)
        .transpose(1, 0, 2)
        .reshape(device_count, vector_entries),
        ((0, 0), (0, vector_tail)),
    ).reshape(device_count, -1, model_width)
    last_term = jnp.concatenate(
        [
            qkv_term.astype(jnp.bfloat16).reshape(device_count, qkv_rows, model_width),
            out_term.astype(jnp.bfloat16).reshape(device_count, out_rows, model_width),
            vector_term.astype(jnp.bfloat16),
        ],
        axis=1,
    )
    last_sum = lax.psum_scatter(
        last_term.reshape(-1, model_width), both, scatter_dimension=0, tiled=True
    ).astype(jnp.float32)
    qkv_grad = last_sum[:qkv_rows]
    out_grad = last_sum[qkv_rows : qkv_rows + out_rows]
    vectors_grad = last_sum[qkv_rows + out_rows :].reshape(-1)[:vector_entries].reshape(vectors.shape)
    qkv_moment_new, qkv_square_new, qkv_weight_new = adam_update(
        qkv_weight, qkv_moment, qkv_square, qkv_grad, rate_matrix, decay_matrix
    )
    out_moment_new, out_square_new, out_weight_new = adam_update(
        out_weight, out_moment, out_square, out_grad, rate_matrix, decay_matrix
    )
    fc_moment_new, fc_square_new, fc_weight_new = adam_update(
        fc_weight, fc_moment, fc_square, fc_grad, rate_matrix, decay_matrix
    )
    proj_moment_new, proj_square_new, proj_weight_new = adam_update(
        proj_weight, proj_moment, proj_square, proj_grad, rate_matrix, decay_matrix
    )
    vectors_moment_new, vectors_square_new, vectors_new = adam_update(
        vectors, vectors_moment, vectors_square, vectors_grad, rate_vector, 0.0
    )
    return (
        layer_out,
        input_grad,
        qkv_grad,
        qkv_moment_new,
        qkv_square_new,
        qkv_weight_new,
        out_grad,
        out_moment_new,
        out_square_new,
        out_weight_new,
        fc_grad,
        fc_moment_new,
        fc_square_new,
        fc_weight_new,
        proj_grad,
        proj_moment_new,
        proj_square_new,
        proj_weight_new,
        vectors_grad,
        vectors_moment_new,
        vectors_square_new,
        vectors_new,
    )


def solution(mesh):
    in_specs = (
        P("batch", "ctx", None),
        P("batch", "ctx", None),
        P("batch", None),
        P(("batch", "ctx"), None),
        P(("batch", "ctx"), None),
        P(("batch", "ctx"), None),
        P(("batch", "ctx"), None),
        P(("batch", "ctx"), None),
        P(("batch", "ctx"), None),
        P(("batch", "ctx"), None),
        P(("batch", "ctx"), None),
        P(("batch", "ctx"), None),
        P(("batch", "ctx"), None),
        P(("batch", "ctx"), None),
        P(("batch", "ctx"), None),
        P(None, ("batch", "ctx")),
        P(None, ("batch", "ctx")),
        P(None, ("batch", "ctx")),
    )
    out_specs = (
        P("batch", "ctx", None),
        P("batch", "ctx", None),
        P(("batch", "ctx"), None),
        P(("batch", "ctx"), None),
        P(("batch", "ctx"), None),
        P(("batch", "ctx"), None),
        P(("batch", "ctx"), None),
        P(("batch", "ctx"), None),
        P(("batch", "ctx"), None),
        P(("batch", "ctx"), None),
        P(("batch", "ctx"), None),
        P(("batch", "ctx"), None),
        P(("batch", "ctx"), None),
        P(("batch", "ctx"), None),
        P(("batch", "ctx"), None),
        P(("batch", "ctx"), None),
        P(("batch", "ctx"), None),
        P(("batch", "ctx"), None),
        P(None, ("batch", "ctx")),
        P(None, ("batch", "ctx")),
        P(None, ("batch", "ctx")),
        P(None, ("batch", "ctx")),
    )
    return jax.shard_map(local, mesh=mesh, in_specs=in_specs, out_specs=out_specs, check_vma=False)
```

time: 953 us -> 617 us (0.65)
  waiting for transfers between devices: 588 us -> 435 us
  blocking collectives: 111 us -> 15.8 us
  matrix products: 127 us -> 43.2 us
  Pallas kernels: 0 us -> 22.5 us
  local copies, waits for them, and re-layouts: 65.5 us -> 46.2 us
  other arithmetic: 40.5 us -> 26.2 us
  starting transfers between devices: 0.9 us -> 12.1 us
    all_gather x8 -> x3, waiting for transfers between devices: 250 us -> 129 us  [the longest x1 64.8 us: local(): first_full = lax.all_gather(first_shard, both, axis=0, tiled=False)]
    reduce_scatter x4 -> x3, waiting for transfers between devices: 338 us -> 225 us  [the longest x1 113 us: local(): lax.psum_scatter(last_term.reshape(-1, model_width), both, scatter_dimens...]
    all_to_all x0 -> x3, waiting for transfers between devices: none -> 79.8 us  [the longest x2 44.8 us: heads_to_tokens(): lax.all_to_all(array.reshape(count, rows, parts * pairs * HD), 'ctx', 0, 0)]
    dot_general x59 -> x3, matrix products: 91.3 us -> 15.2 us  [the longest x1 6.4 us: local(): mlp_out = jnp.dot(active_low, proj_full, preferred_element_type=jnp.float32)]
    all_gather x3 -> x0, blocking collectives: 71.4 us -> none  [the longest x1 43.9 us: local(): lax.all_gather(vectors.astype(jnp.bfloat16), ('batch', 'ctx'), axis=1, ti...]
    dynamic_slice x40 -> x0, local copies, waits for them, and re-layouts: 40.2 us -> none  [the longest x8 15.4 us: query_inner_step(): lax.dynamic_slice_in_dim(query_value_piece, offset, query_sub_rows, 1)]
    unnamed x1 -> x0, blocking collectives: 39.9 us -> none
    pallas_call x0 -> x2, Pallas kernels: none -> 22.5 us  [the longest x1 13.2 us: attention_backward(): pl.pallas_call(functools.partial(attention_backward_kernel, pairs, length...]
  transfers between devices with their start and end apart: 12 -> 9, of which waited for: 9 -> 8; matrix products, arithmetic and copies ran while one was open for 22% -> 11% of each run, Pallas kernels for 0% -> 4%
where the time goes in v1:
time: 617 us; the launch traced here: 616 us
  waiting for transfers between devices  435 us (71%)
  local copies, waits for them, and re-layouts  46.2 us (7%)
  matrix products  43.2 us (7%)
  other arithmetic  26.2 us (4%)
  Pallas kernels  22.5 us (4%)
  blocking collectives  15.8 us (3%)
  between operations  15.2 us (2%)
  starting transfers between devices  12.1 us (2%)
    reduce_scatter x1, waiting for transfers between devices, local(): lax.psum_scatter(last_term.reshape(-1, model_width), both, scatter_dimens...  113 us
    reduce_scatter x1, waiting for transfers between devices, local(): lax.psum_scatter(dot_cols(active_low, grad_top).astype(jnp.bfloat16), bot...  105 us
    all_gather x1, waiting for transfers between devices, local(): first_full = lax.all_gather(first_shard, both, axis=0, tiled=False)  64.8 us
    all_gather x1, waiting for transfers between devices, local(): lax.all_gather(proj_weight.astype(jnp.bfloat16), both, axis=0, tiled=True)  64.5 us
    all_to_all x2, waiting for transfers between devices, heads_to_tokens(): lax.all_to_all(array.reshape(count, rows, parts * pairs * HD), 'ctx', 0, 0)  44.8 us
    all_to_all x1, waiting for transfers between devices, tokens_to_heads(): array = lax.all_to_all(array, 'ctx', 0, 0)  34.9 us
    all_to_all x1, blocking collectives, tokens_to_heads(): array = lax.all_to_all(array, 'ctx', 0, 0)  15.8 us
    dot_general x4, matrix products, dot_cols(): lax.dot_general(left, right, (((0,), (0,)), ((), ())), preferred_element_...  13.3 us
  transfers between devices with their start and end apart: 9, of which 8 were waited for; matrix products, arithmetic and copies ran while one was open for 11% of the time, Pallas kernels for 4%

profile of v1, /device:TPU:0, one launch (start us, length us, event | category | flops | bytes accessed | tf_op | source)
XLA Modules:
  0.0 615.6 jit_solution(3246964214898546655)
XLA Ops:
  8.1 0.9 convert_bitcast_fusion.2
  9.0 0.9 convert_bitcast_fusion.1
  10.7 1.6 convert_element_type.127
  12.4 1.1 convert_reduce_fusion
  14.1 1.2 multiply_reduce_fusion.5
  15.9 64.8 %all-gather.4.cloned.1.call-done = bf16[32,112,768]{2,1,0:T(8,128)(2,1)} async-done(((bf16[1,112,768]{2,1,0:T(8,128)(2,1)}), bf16[32,112,768]{2,1,0:T(8,128)(2,1)}) %all-gather.4.cloned.1.call-update) | async-done | bytes 5505040 | tf_op jit(solution)/shard_map/all_gather | solution.py:256
  80.6 2.1 slice.99
  82.7 3.0 copy.91
  87.7 2.3 slice.103
  90.3 1.4 copy-done.16
  91.9 1.1 fusion
  94.2 1.1 copy.98
  95.4 4.3 all-to-all-start
  100.6 34.9 %all-to-all-done = bf16[8,128,576]{1,2,0:T(8,128)(2,1)} async-done(((bf16[8,128,576]{1,2,0:T(8,128)(2,1)}), bf16[8,128,576]{1,2,0:T(8,128)(2,1)}, u32[]{:S(2)}, u32[]{:S(2)}) %all-to-all-start) | async-done | bytes 1179680 | tf_op jit(solution)/shard_map/all_to_all | solution.py:197
  135.6 1.7 copy.99
  137.3 9.4 %attention_forward.1 = (bf16[1024,192]{1,0:T(8,128)(2,1)S(1)}, f32[1024,192]{1,0:T(8,128)S(1)}, f32[1024,3]{1,0:T(8,128)S(1)}) custom-call(bf16[1024,576]{1,0:T(8,128)(2,1)S(1)} %bitcast.115, bf16[1024,576]{1,0:T(8,128)(2,1)S(1)} %bitcast.116, s32[1024,3]{1,0:T(8,128)S(1)} %copy.101.low_ref, s32[1024,1]{1,0:T(8,128)S(1)} %fusion.23.qpos_ref, ...), custom_call_target="tpu_custom_call" | custom-call | tf_op jit(solution)/shard_map/attention_forward/pallas_call | solution.py:145
  146.7 1.0 copy-done.3
  147.7 1.0 copy.102
  148.6 3.6 all-to-all-start.1
  152.9 2.4 slice.106
  155.3 9.6 %all-to-all-done.1 = bf16[8,128,192]{1,2,0:T(8,128)(2,1)S(1)} async-done(((bf16[8,128,192]{1,2,0:T(8,128)(2,1)}), bf16[8,128,192]{1,2,0:T(8,128)(2,1)S(1)}, u32[]{:S(2)}, u32[]{:S(2)}) %all-to-all-start.1) | async-done | bytes 393248 | tf_op jit(solution)/shard_map/all_to_all | solution.py:203
  165.0 0.7 copy-done.23
  165.7 1.4 copy.103
  167.1 2.8 fusion.70
  169.9 1.4 multiply_reduce_fusion.4
  171.3 4.1 convolution_add_fusion.1
  175.5 1.7 copy-done.59
  177.1 4.4 convolution_convert_fusion
  181.8 104.8 %reduce-scatter.8.cloned.1.call-done = bf16[96,768]{1,0:T(8,128)(2,1)} async-done(((bf16[3072,768]{1,0:T(8,128)(2,1)}), bf16[96,768]{1,0:T(8,128)(2,1)}) %reduce-scatter.8.cloned.1.call-update) | async-done | bytes 147472 | tf_op jit(solution)/shard_map/reduce_scatter | solution.py:297
  286.6 2.0 multiply_subtract_fusion
  288.7 64.5 %all-gather.8.cloned.1.call-done = bf16[3072,768]{1,0:T(8,128)(2,1)} async-done(((bf16[96,768]{1,0:T(8,128)(2,1)}), bf16[3072,768]{1,0:T(8,128)(2,1)}) %all-gather.8.cloned.1.call-update) | async-done | bytes 4718608 | tf_op jit(solution)/shard_map/all_gather | solution.py:258
  353.3 6.2 %fusion.65 = (bf16[3072]{0:T(1024)(128)(2,1)S(1)}, bf16[256,3072]{1,0:T(8,128)(2,1)S(1)}) fusion(f32[256,3072]{1,0:T(8,128)} %copy-done.59, bf16[256,768]{1,0:T(8,128)(2,1)} %bitcast.146, bf16[3072,768]{1,0:T(8,128)(2,1)} %all-gather.8.cloned.1.call-done), kind=kOutput, calls=%fused_computation.157 | convolution fusion | flops 1224471552 | bytes 9836544 | tf_op jit(solution)/shard_map/dot_general | solution.py:45
  359.5 4.8 convolution_convert_fusion.1
  364.3 5.5 multiply_reduce_fusion
  369.9 1.1 copy-done.28
  371.0 1.5 fusion.68
  372.4 1.2 fusion.67
  374.5 15.8 %all_to_all.20 = bf16[8,128,192]{1,2,0:T(8,128)(2,1)S(1)} all-to-all(bf16[8,128,192]{1,2,0:T(8,128)(2,1)S(1)} %bitcast.145), channel_id=1, replica_groups=mesh['batch'=4,'ctx'=8] {'ctx'}, dimensions={0} | all-to-all | bytes 786432 | tf_op jit(solution)/shard_map/all_to_all | solution.py:197
  390.3 1.0 copy.111
  391.3 1.0 copy-done.1
  392.4 1.0 copy-done.2
  393.4 1.2 copy-done.4
  394.7 1.0 copy-done.6
  395.7 13.2 %attention_backward.1 = bf16[1024,576]{1,0:T(8,128)(2,1)S(1)} custom-call(bf16[1024,576]{1,0:T(8,128)(2,1)S(1)} %bitcast.117, bf16[1024,576]{1,0:T(8,128)(2,1)S(1)} %bitcast.118, s32[1024,3]{1,0:T(8,128)S(1)} %copy.101.low_ref, s32[1024,1]{1,0:T(8,128)S(1)} %copy-done.1, s32[1,1024]{1,0:T(1,128)S(1)} %fusion.45.kpos_ref, f32[1024,192]{1,0:T(8,128)S(1)} %copy-done.4, ...), custom_call_target="tpu_custom_call" | custom-call | tf_op jit(solution)/shard_map/attention_backward/pallas_call | solution.py:168
  408.9 1.4 copy.113
  410.4 3.6 all-to-all-start.3
  415.7 1.4 concatenate.56
  417.1 1.4 concatenate.57
  419.2 1.5 convolution_convert_fusion.3
  420.7 35.2 %all-to-all-done.3 = bf16[8,128,576]{1,2,0:T(8,128)(2,1)S(1)} async-done(((bf16[8,128,576]{1,2,0:T(8,128)(2,1)}), bf16[8,128,576]{1,2,0:T(8,128)(2,1)S(1)}, u32[]{:S(2)}, u32[]{:S(2)}) %all-to-all-start.3) | async-done | bytes 1179680 | tf_op jit(solution)/shard_map/all_to_all | solution.py:203
  456.0 1.2 copy.115
  457.7 3.3 fusion.59
  461.1 1.0 multiply_reduce_fusion.1
  463.4 1.3 pad.11
  464.7 2.5 copy.117
  467.2 2.6 convolution_convert_fusion.2
  469.8 2.9 pad_maximum_fusion
  473.7 6.4 %fusion.10 = bf16[256,768]{1,0:T(8,128)(2,1)} fusion(f32[256,768]{1,0:T(8,128)} %get-tuple-element.77, bf16[3072,768]{1,0:T(8,128)(2,1)} %all-gather.8.cloned.1.call-done, f32[768]{0:T(1024)S(1)} %add.342, f32[256,3072]{1,0:T(8,128)} %copy-done.59), kind=kOutput, calls=%fused_computation.22 | convolution fusion | flops 1215627264 | bytes 9047040 | tf_op jit(solution)/shard_map/dot_general | solution.py:289
  480.3 1.1 add_convert_fusion
  481.3 7.5 %reduce-scatter.6.cloned.1.call-done = bf16[96,768]{1,0:T(8,128)(2,1)} async-done(((bf16[3072,768]{1,0:T(8,128)(2,1)}), bf16[96,768]{1,0:T(8,128)(2,1)}) %reduce-scatter.6.cloned.1.call-update) | async-done | bytes 147472 | tf_op jit(solution)/shard_map/reduce_scatter | solution.py:303
  488.8 2.0 multiply_subtract_fusion.1
  490.8 113.0 %reduce-scatter.4.cloned.1.call-done = bf16[112,768]{1,0:T(8,128)(2,1)} async-done(((bf16[3584,768]{1,0:T(8,128)(2,1)}), bf16[112,768]{1,0:T(8,128)(2,1)}) %reduce-scatter.4.cloned.1.call-update) | async-done | bytes 172048 | tf_op jit(solution)/shard_map/reduce_scatter | solution.py:364
  605.4 1.9 multiply_subtract_fusion.2
  607.3 1.5 multiply_subtract_fusion.3
  (204 shorter events, 16.0 us)
Async XLA Ops:
  7.2 73.4 %all-gather.4.cloned.1.call-start = ((), (), s32[]{:S(2)}) async-start(), calls=%async_computation.7 | async-start | bytes 5677056 | tf_op jit(solution)/shard_map/all_gather | solution.py:256
  10.6 160.7 %all-gather.6.cloned.1.call-start = ((), (), s32[]{:S(2)}) async-start(), calls=%async_computation.8 | async-start | bytes 4866048 | tf_op jit(solution)/shard_map/all_gather | solution.py:257
  87.6 2.3 copy-start.10
  89.9 1.8 copy-start.16
  90.2 1.6 copy-start.20
  93.9 5.7 copy-start.58
  95.4 40.2 %all-to-all-start = ((bf16[8,128,576]{1,2,0:T(8,128)(2,1)}), bf16[8,128,576]{1,2,0:T(8,128)(2,1)}, u32[]{:S(2)}, u32[]{:S(2)}) async-start(bf16[8,128,576]{1,2,0:T(8,128)(2,1)} %bitcast.12), calls=%async_computation | async-start | bytes 2359296 | tf_op jit(solution)/shard_map/all_to_all | solution.py:197
  100.6 48.0 %copy-start = (s32[1024,1]{1,0:T(8,128)}, s32[1024,1]{1,0:T(8,128)S(1)}, u32[]{:S(2)}) copy-start(s32[1024,1]{1,0:T(8,128)S(1)} %fusion.23.qpos_ref) | copy-start | bytes 12292
  137.3 15.2 %slice-start = ((f32[12,32,24]{1,2,0:T(8,128)}), f32[4,32,24]{1,2,0:T(8,128)S(1)}, s32[]{:S(2)}) async-start(f32[12,32,24]{1,2,0:T(8,128)} %copy-done.29), calls=%async_computation.13 | async-start | bytes 98304 | tf_op jit(solution)/shard_map/slice | solution.py:286
  147.7 22.3 %copy-start.5 = (f32[1024,3]{1,0:T(8,128)}, f32[1024,3]{1,0:T(8,128)S(1)}, u32[]{:S(2)}) copy-start(f32[1024,3]{1,0:T(8,128)S(1)} %get-tuple-element.27.lse_ref) | copy-start | bytes 36868
  148.6 18.5 %copy-start.11 = (bf16[2,128,768]{2,1,0:T(8,128)(2,1)S(1)}, bf16[2,128,768]{2,1,0:T(8,128)(2,1)}, u32[]{:S(2)}) copy-start(bf16[2,128,768]{2,1,0:T(8,128)(2,1)} %param.18) | copy-start | bytes 1179652
  148.6 16.3 %all-to-all-start.1 = ((bf16[8,128,192]{1,2,0:T(8,128)(2,1)}), bf16[8,128,192]{1,2,0:T(8,128)(2,1)S(1)}, u32[]{:S(2)}, u32[]{:S(2)}) async-start(bf16[8,128,192]{1,2,0:T(8,128)(2,1)} %copy.102), calls=%async_computation.1 | async-start | bytes 786432 | tf_op jit(solution)/shard_map/all_to_all | solution.py:203
  152.2 134.4 %reduce-scatter.8.cloned.1.call-start = ((), (), s32[]{:S(2)}) async-start(), calls=%async_computation.12 | async-start | bytes 4866048 | tf_op jit(solution)/shard_map/reduce_scatter | solution.py:297
  167.1 8.3 %copy-start.21 = (bf16[2,128,1,12,64]{1,0,4,3,2:T(2,128)(2,1)}, bf16[2,128,1,12,64]{1,0,4,3,2:T(2,128)(2,1)S(1)}, u32[]{:S(2)}) copy-start(bf16[2,128,1,12,64]{1,0,4,3,2:T(2,128)(2,1)S(1)} %copy.103) | copy-start | bytes 1179652
  171.3 5.8 copy-start.24
  175.4 1.7 copy-start.59
  181.5 105.1 %copy-start.30 = (f32[96,768]{1,0:T(8,128)S(1)}, f32[96,768]{1,0:T(8,128)}, u32[]{:S(2)}) copy-start(f32[96,768]{1,0:T(8,128)} %param.30) | copy-start | bytes 884740
  181.5 105.1 %copy-start.31 = (f32[96,768]{1,0:T(8,128)S(1)}, f32[96,768]{1,0:T(8,128)}, u32[]{:S(2)}) copy-start(f32[96,768]{1,0:T(8,128)} %param.32) | copy-start | bytes 884740
  181.5 105.1 %copy-start.32 = (f32[96,768]{1,0:T(8,128)S(1)}, f32[96,768]{1,0:T(8,128)}, u32[]{:S(2)}) copy-start(f32[96,768]{1,0:T(8,128)} %param.31) | copy-start | bytes 884740
  181.5 171.7 %all-gather.8.cloned.1.call-start = ((), (), s32[]{:S(2)}) async-start(), calls=%async_computation.9 | async-start | bytes 4866048 | tf_op jit(solution)/shard_map/all_gather | solution.py:258
  288.7 200.2 %reduce-scatter.6.cloned.1.call-start = ((), (), s32[]{:S(2)}) async-start(), calls=%async_computation.11 | async-start | bytes 4866048 | tf_op jit(solution)/shard_map/reduce_scatter | solution.py:303
  369.8 1.1 copy-start.28
  369.9 3.8 copy-start.14
  373.6 17.7 %copy-start.7 = (f32[256,768]{1,0:T(8,128)}, f32[256,768]{1,0:T(8,128)S(1)}, u32[]{:S(2)}) copy-start(f32[256,768]{1,0:T(8,128)S(1)} %get-tuple-element.60) | copy-start | bytes 2359300
  391.3 1.1 copy-start.1
  392.4 1.1 copy-start.2
  393.4 1.2 copy-start.4
  408.9 5.3 copy-start.25
  408.9 10.3 %copy-start.8 = (f32[256,768]{1,0:T(8,128)S(1)}, f32[256,768]{1,0:T(8,128)}, u32[]{:S(2)}) copy-start(f32[256,768]{1,0:T(8,128)} %copy-done.7) | copy-start | bytes 2359300
  408.9 10.3 %copy-start.22 = (bf16[2,128,1,12,64]{1,0,4,3,2:T(2,128)(2,1)S(1)}, bf16[2,128,1,12,64]{1,0,4,3,2:T(2,128)(2,1)}, u32[]{:S(2)}) copy-start(bf16[2,128,1,12,64]{1,0,4,3,2:T(2,128)(2,1)} %copy-done.21) | copy-start | bytes 1179652
  410.4 45.5 %all-to-all-start.3 = ((bf16[8,128,576]{1,2,0:T(8,128)(2,1)}), bf16[8,128,576]{1,2,0:T(8,128)(2,1)S(1)}, u32[]{:S(2)}, u32[]{:S(2)}) async-start(bf16[8,128,576]{1,2,0:T(8,128)(2,1)} %copy.113), calls=%async_computation.3 | async-start | bytes 2359296 | tf_op jit(solution)/shard_map/all_to_all | solution.py:203
  413.9 189.9 %reduce-scatter.4.cloned.1.call-start = ((), (), s32[]{:S(2)}) async-start(), calls=%async_computation.10 | async-start | bytes 5677056 | tf_op jit(solution)/shard_map/reduce_scatter | solution.py:364
  420.7 37.0 %copy-start.12 = (bf16[2,128,768]{2,1,0:T(8,128)(2,1)S(1)}, bf16[2,128,768]{2,1,0:T(8,128)(2,1)}, u32[]{:S(2)}) copy-start(bf16[2,128,768]{2,1,0:T(8,128)(2,1)} %param.18) | copy-start | bytes 1179652
  457.2 6.2 %copy-start.13 = (bf16[2,128,3,12,64]{1,0,4,3,2:T(2,128)(2,1)}, bf16[2,128,3,12,64]{1,0,4,3,2:T(2,128)(2,1)S(1)}, u32[]{:S(2)}) copy-start(bf16[2,128,3,12,64]{1,0,4,3,2:T(2,128)(2,1)S(1)} %copy.115) | copy-start | bytes 3538948
  457.6 3.4 copy-start.54
  457.6 3.4 copy-start.47
  457.7 4.9 copy-start.45
  457.7 4.9 copy-start.43
  457.7 4.9 copy-start.44
  457.7 4.9 copy-start.42
  457.7 4.9 copy-start.38
  461.0 2.4 copy-start.17
  461.0 1.1 copy-start.49
  461.0 1.4 copy-start.51
  467.2 2.6 copy-start.15
  467.2 2.6 copy-start.19
  473.6 6.5 %copy-start.57 = (f32[256]{0:T(256)S(1)}, f32[256]{0:T(256)}, u32[]{:S(2)}) copy-start(f32[256]{0:T(256)} %get-tuple-element.31) | copy-start | bytes 3076
  473.6 6.6 %copy-start.9 = (f32[256,768]{1,0:T(8,128)S(1)}, f32[256,768]{1,0:T(8,128)}, u32[]{:S(2)}) copy-start(f32[256,768]{1,0:T(8,128)} %copy-done.7) | copy-start | bytes 2359300
  473.6 6.6 %copy-start.18 = (f32[256,768]{1,0:T(8,128)S(1)}, f32[256,768]{1,0:T(8,128)}, u32[]{:S(2)}) copy-start(f32[256,768]{1,0:T(8,128)} %copy-done.17) | copy-start | bytes 2359300
  473.6 6.6 %copy-start.48 = (f32[256]{0:T(256)S(1)}, f32[256]{0:T(256)}, u32[]{:S(2)}) copy-start(f32[256]{0:T(256)} %get-tuple-element.74) | copy-start | bytes 3076
  473.6 6.6 %copy-start.50 = (f32[256]{0:T(256)S(1)}, f32[256]{0:T(256)}, u32[]{:S(2)}) copy-start(f32[256]{0:T(256)} %copy-done.49) | copy-start | bytes 3076
  473.7 6.6 %copy-start.52 = (f32[256]{0:T(256)S(1)}, f32[256]{0:T(256)}, u32[]{:S(2)}) copy-start(f32[256]{0:T(256)} %copy-done.51) | copy-start | bytes 3076
  473.7 15.1 %copy-start.26 = (f32[96,768]{1,0:T(8,128)S(1)}, f32[96,768]{1,0:T(8,128)}, u32[]{:S(2)}) copy-start(f32[96,768]{1,0:T(8,128)} %param.27) | copy-start | bytes 884740
  473.7 15.1 %copy-start.33 = (f32[96,768]{1,0:T(8,128)S(1)}, f32[96,768]{1,0:T(8,128)}, u32[]{:S(2)}) copy-start(f32[96,768]{1,0:T(8,128)} %param.29) | copy-start | bytes 884740
  473.7 15.1 %copy-start.34 = (f32[96,768]{1,0:T(8,128)S(1)}, f32[96,768]{1,0:T(8,128)}, u32[]{:S(2)}) copy-start(f32[96,768]{1,0:T(8,128)} %param.28) | copy-start | bytes 884740
  480.1 124.6 %copy-start.46 = (f32[12,24]{1,0:T(8,128)S(1)}, f32[12,24]{1,0:T(8,128)}, u32[]{:S(2)}) copy-start(f32[12,24]{1,0:T(8,128)} %param.33) | copy-start | bytes 3460
  480.1 124.6 %copy-start.55 = (f32[12,24]{1,0:T(8,128)S(1)}, f32[12,24]{1,0:T(8,128)}, u32[]{:S(2)}) copy-start(f32[12,24]{1,0:T(8,128)} %param.35) | copy-start | bytes 3460
  480.1 124.7 %copy-start.56 = (f32[12,24]{1,0:T(8,128)S(1)}, f32[12,24]{1,0:T(8,128)}, u32[]{:S(2)}) copy-start(f32[12,24]{1,0:T(8,128)} %param.34) | copy-start | bytes 3460
  480.1 125.3 %copy-start.27 = (f32[72,768]{1,0:T(8,128)S(1)}, f32[72,768]{1,0:T(8,128)}, u32[]{:S(2)}) copy-start(f32[72,768]{1,0:T(8,128)} %param.21) | copy-start | bytes 663556
  480.1 125.3 %copy-start.36 = (f32[72,768]{1,0:T(8,128)S(1)}, f32[72,768]{1,0:T(8,128)}, u32[]{:S(2)}) copy-start(f32[72,768]{1,0:T(8,128)} %param.23) | copy-start | bytes 663556
  480.1 125.3 %copy-start.37 = (f32[72,768]{1,0:T(8,128)S(1)}, f32[72,768]{1,0:T(8,128)}, u32[]{:S(2)}) copy-start(f32[72,768]{1,0:T(8,128)} %param.22) | copy-start | bytes 663556
  480.2 127.0 %copy-start.35 = (f32[24,768]{1,0:T(8,128)S(1)}, f32[24,768]{1,0:T(8,128)}, u32[]{:S(2)}) copy-start(f32[24,768]{1,0:T(8,128)} %param.24) | copy-start | bytes 221188
  480.2 127.0 %copy-start.39 = (f32[24,768]{1,0:T(8,128)S(1)}, f32[24,768]{1,0:T(8,128)}, u32[]{:S(2)}) copy-start(f32[24,768]{1,0:T(8,128)} %param.26) | copy-start | bytes 221188
  480.2 127.0 %copy-start.40 = (f32[24,768]{1,0:T(8,128)S(1)}, f32[24,768]{1,0:T(8,128)}, u32[]{:S(2)}) copy-start(f32[24,768]{1,0:T(8,128)} %param.25) | copy-start | bytes 221188
  (6 other events, 4.7 us)
Sparse Core Ops, SparseCore 0:
  11.6 68.9 all-gather.3
  84.2 73.3 all-gather.5
  181.7 104.8 reduce-scatter.7
  290.5 62.7 all-gather.7
  370.0 118.7 reduce-scatter.5
  494.2 109.5 reduce-scatter.3

commit v2 on v1

--- a/solution.py
+++ b/solution.py
@@ -205,6 +205,115 @@
     array = array.reshape(count * pairs, rows, parts, HD)[: groups * H]
     array = array.reshape(groups, H, rows, parts, HD).transpose(0, 2, 3, 1, 4)
     return array.reshape(groups * rows, parts * H * HD)
+
+
+grid_orders = ((4, 1, 0, 3, 2), (4, 0, 3, 2, 1), (4, 3, 2, 1, 0))
+
+
+def drop_axis(index, axis, bit):
+    return index[:axis] + (bit,) + index[axis:]
+
+
+def scatter_sum_kernel(*refs):
+    terms, sums = refs[:3], refs[3:6]
+    landed = [refs[6 + 5 * part : 11 + 5 * part] for part in range(3)]
+    send_sem, recv_sem = refs[21:]
+    batch, ctx = lax.axis_index("batch"), lax.axis_index("ctx")
+    bits = (
+        lax.div(batch, 2),
+        lax.rem(batch, 2),
+        lax.div(ctx, 4),
+        lax.rem(lax.div(ctx, 2), 2),
+        lax.rem(ctx, 2),
+    )
+    partners = (
+        (batch + 2 - 4 * bits[0], ctx),
+        (batch + 1 - 2 * bits[1], ctx),
+        (batch, ctx + 4 - 8 * bits[2]),
+        (batch, ctx + 2 - 4 * bits[3]),
+        (batch, ctx + 1 - 2 * bits[4]),
+    )
+    barrier = pltpu.get_barrier_semaphore()
+    for partner in partners:
+        pl.semaphore_signal(
+            barrier, inc=1, device_id=partner, device_id_type=pl.DeviceIdType.MESH
+        )
+    pl.semaphore_wait(barrier, 5)
+
+    def place(part, stage):
+        axis = grid_orders[part][stage]
+        return axis, sum(1 for earlier in grid_orders[part][:stage] if earlier < axis)
+
+    def begin(part, stage):
+        axis, gone = place(part, stage)
+        source = terms[part] if stage == 0 else landed[part][stage - 1]
+        lead = (slice(None),) * (axis - gone)
+        copy = pltpu.make_async_remote_copy(
+            src_ref=source.at[lead + (1 - bits[axis],)],
+            dst_ref=landed[part][stage],
+            send_sem=send_sem.at[part, stage],
+            recv_sem=recv_sem.at[part, stage],
+            device_id=partners[axis],
+            device_id_type=pl.DeviceIdType.MESH,
+        )
+        copy.start()
+        return copy
+
+    copies = {(part, 0): begin(part, 0) for part in range(3)}
+    for stage in range(5):
+        for part in range(3):
+            axis, gone = place(part, stage)
+            source = terms[part] if stage == 0 else landed[part][stage - 1]
+            target = landed[part][stage]
+            copies[part, stage].wait_recv()
+            left = 4 - stage
+            if left:
+
+                @pl.loop(0, 2**left)
+                def _(turn):
+                    index = tuple(
+                        lax.rem(lax.div(turn, 2 ** (left - 1 - level)), 2) for level in range(left)
+                    )
+                    target[index] = target[index] + source[drop_axis(index, axis - gone, bits[axis])]
+
+                copies[part, stage + 1] = begin(part, stage + 1)
+            else:
+                sums[part][...] = target[...].astype(jnp.float32) + source[bits[axis]].astype(
+                    jnp.float32
+                )
+    for copy in copies.values():
+        copy.wait_send()
+
+
+def scatter_sums(terms):
+    batch_count, ctx_count = lax.axis_size("batch"), lax.axis_size("ctx")
+    devices = batch_count * ctx_count
+    rows = [term.shape[0] // devices for term in terms]
+    width = terms[0].shape[1]
+    if (batch_count, ctx_count) != (4, 8) or any(count % 16 for count in rows):
+        return [
+            lax.psum_scatter(
+                term, ("batch", "ctx"), scatter_dimension=0, tiled=True
+            ).astype(jnp.float32)
+            for term in terms
+        ]
+    whole = pl.BlockSpec(memory_space=pltpu.VMEM)
+    return pl.pallas_call(
+        scatter_sum_kernel,
+        in_specs=[whole] * 3,
+        out_specs=[whole] * 3,
+        out_shape=[jax.ShapeDtypeStruct((count, width), jnp.float32) for count in rows],
+        scratch_shapes=[
+            pltpu.VMEM((2,) * (4 - stage) + (count, width), jnp.bfloat16)
+            for count in rows
+            for stage in range(5)
+        ]
+        + [pltpu.SemaphoreType.DMA((3, 5)), pltpu.SemaphoreType.DMA((3, 5))],
+        compiler_params=pltpu.CompilerParams(
+            collective_id=0, has_side_effects=True, vmem_limit_bytes=52 * 2**20
+        ),
+        name="scatter_sum",
+    )(*[term.reshape((2,) * 5 + (count, width)) for term, count in zip(terms, rows)])
 
 
 def local(
@@ -294,18 +403,11 @@
     )
     grad_top = cotangent.reshape(total_rows, model_width)
     grad_top_f = grad_top.astype(jnp.float32)
-    proj_grad = lax.psum_scatter(
-        dot_cols(active_low, grad_top).astype(jnp.bfloat16), both, scatter_dimension=0, tiled=True
-    ).astype(jnp.float32)
+    proj_term = dot_cols(active_low, grad_top).astype(jnp.bfloat16)
     grad_active = dot_rows(grad_top, proj_full)
     unused, pullback = jax.vjp(gelu_tanh, before)
     grad_before = pullback(grad_active)[0].astype(jnp.bfloat16)
-    fc_grad = lax.psum_scatter(
-        dot_cols(grad_before, hidden_two_low).astype(jnp.bfloat16),
-        both,
-        scatter_dimension=0,
-        tiled=True,
-    ).astype(jnp.float32)
+    fc_term = dot_cols(grad_before, hidden_two_low).astype(jnp.bfloat16)
     grad_hidden_two = jnp.dot(grad_before, fc_full, preferred_element_type=jnp.float32)
     unused, pull_two = jax.vjp(norm_layer, middle, vector_rows[5], vector_rows[6])
     grad_middle_norm, grad_gain_two, grad_bias_two = pull_two(grad_hidden_two)
@@ -361,9 +463,9 @@
         ],
         axis=1,
     )
-    last_sum = lax.psum_scatter(
-        last_term.reshape(-1, model_width), both, scatter_dimension=0, tiled=True
-    ).astype(jnp.float32)
+    last_sum, fc_grad, proj_grad = scatter_sums(
+        [last_term.reshape(-1, model_width), fc_term, proj_term]
+    )
     qkv_grad = last_sum[:qkv_rows]
     out_grad = last_sum[qkv_rows : qkv_rows + out_rows]
     vectors_grad = last_sum[qkv_rows + out_rows :].reshape(-1)[:vector_entries].reshape(vectors.shape)

time: 617 us -> 453 us (0.73)
  waiting for transfers between devices: 435 us -> 166 us
  Pallas kernels: 22.5 us -> 117 us
  local copies, waits for them, and re-layouts: 46.2 us -> 58.5 us
    reduce_scatter x3 -> x0, waiting for transfers between devices: 225 us -> none  [the longest x1 113 us: local(): lax.psum_scatter(last_term.reshape(-1, model_width), both, scatter_dimens...]
    pallas_call x0 -> x1, Pallas kernels: none -> 94.1 us  [scatter_sums(): pl.pallas_call(scatter_sum_kernel, in_specs=[whole] * 3, out_specs=[whole...]
    all_gather x1, waiting for transfers between devices: 64.5 us -> 5.42 us  [local(): lax.all_gather(proj_weight.astype(jnp.bfloat16), both, axis=0, tiled=True)]
    all_gather x1, waiting for transfers between devices: 0.02 us -> 54.6 us  [local(): lax.all_gather(fc_weight.astype(jnp.bfloat16), both, axis=0, tiled=True)]
    all_to_all x2, waiting for transfers between devices: 44.8 us -> 7.68 us  [heads_to_tokens(): lax.all_to_all(array.reshape(count, rows, parts * pairs * HD), 'ctx', 0, 0)]
    unnamed x128 -> x120, local copies, waits for them, and re-layouts: 12.7 us -> 21.1 us
    concatenate x10, local copies, waits for them, and re-layouts: 5.23 us -> 11.9 us  [local(): jnp.concatenate([jnp.stack([grad_gain_one, grad_bias_one, mixed_sums[:mod...]
  transfers between devices with their start and end apart: 9 -> 6, of which waited for: 8 -> 5; matrix products, arithmetic and copies ran while one was open for 11% -> 12% of each run, Pallas kernels for 4% -> 2%
where the time goes in v2:
time: 453 us; the launch traced here: 451 us
  waiting for transfers between devices  166 us (37%)
  Pallas kernels  117 us (26%)
  local copies, waits for them, and re-layouts  58.5 us (13%)
  matrix products  42.2 us (9%)
  other arithmetic  25.3 us (6%)
  blocking collectives  15.8 us (3%)
  between operations  14.6 us (3%)
  starting transfers between devices  11.9 us (3%)
    pallas_call x1, Pallas kernels, scatter_sums(): pl.pallas_call(scatter_sum_kernel, in_specs=[whole] * 3, out_specs=[whole...  94.1 us
    all_gather x1, waiting for transfers between devices, local(): first_full = lax.all_gather(first_shard, both, axis=0, tiled=False)  63 us
    all_gather x1, waiting for transfers between devices, local(): lax.all_gather(fc_weight.astype(jnp.bfloat16), both, axis=0, tiled=True)  54.6 us
    all_to_all x1, waiting for transfers between devices, tokens_to_heads(): array = lax.all_to_all(array, 'ctx', 0, 0)  35.1 us
    unnamed x120, local copies, waits for them, and re-layouts  21.1 us
    dot_general x4, matrix products, dot_rows(): lax.dot_general(left, right, (((1,), (1,)), ((), ())), preferred_element_...  16.3 us
    all_to_all x1, blocking collectives, tokens_to_heads(): array = lax.all_to_all(array, 'ctx', 0, 0)  15.8 us
    dot_general x4, matrix products, dot_cols(): lax.dot_general(left, right, (((0,), (0,)), ((), ())), preferred_element_...  13.6 us
  transfers between devices with their start and end apart: 6, of which 5 were waited for; matrix products, arithmetic and copies ran while one was open for 12% of the time, Pallas kernels for 2%

profile of v2, /device:TPU:0, one launch (start us, length us, event | category | flops | bytes accessed | tf_op | source)
XLA Modules:
  0.0 450.9 jit_solution(6220575239143470023)
XLA Ops:
  10.7 1.6 convert_element_type.121
  12.4 1.6 convert_element_type.119
  14.1 1.1 convert_reduce_fusion
  15.8 1.2 multiply_reduce_fusion.5
  17.6 63.0 %all-gather.4.cloned.1.call-done = bf16[32,112,768]{2,1,0:T(8,128)(2,1)} async-done(((bf16[1,112,768]{2,1,0:T(8,128)(2,1)}), bf16[32,112,768]{2,1,0:T(8,128)(2,1)}) %all-gather.4.cloned.1.call-update) | async-done | bytes 5505040 | tf_op jit(solution)/shard_map/all_gather | solution.py:365
  80.6 2.1 slice.99
  82.7 3.0 copy.91
  87.1 2.3 slice.103
  89.7 1.4 copy-done.20
  91.3 1.1 fusion
  93.7 1.2 copy.98
  94.8 4.3 all-to-all-start
  100.1 35.1 %all-to-all-done = bf16[8,128,576]{1,2,0:T(8,128)(2,1)} async-done(((bf16[8,128,576]{1,2,0:T(8,128)(2,1)}), bf16[8,128,576]{1,2,0:T(8,128)(2,1)}, u32[]{:S(2)}, u32[]{:S(2)}) %all-to-all-start) | async-done | bytes 1179680 | tf_op jit(solution)/shard_map/all_to_all | solution.py:197
  135.2 1.7 copy.99
  136.9 9.4 %attention_forward.1 = (bf16[1024,192]{1,0:T(8,128)(2,1)S(1)}, f32[1024,192]{1,0:T(8,128)S(1)}, f32[1024,3]{1,0:T(8,128)S(1)}) custom-call(bf16[1024,576]{1,0:T(8,128)(2,1)S(1)} %bitcast.118, bf16[1024,576]{1,0:T(8,128)(2,1)S(1)} %bitcast.119, s32[1024,3]{1,0:T(8,128)S(1)} %copy.101.low_ref, s32[1024,1]{1,0:T(8,128)S(1)} %fusion.23.qpos_ref, ...), custom_call_target="tpu_custom_call" | custom-call | tf_op jit(solution)/shard_map/attention_forward/pallas_call | solution.py:145
  148.2 3.6 all-to-all-start.1
  151.9 5.4 %all-gather.8.cloned.1.call-done = bf16[3072,768]{1,0:T(8,128)(2,1)} async-done(((bf16[96,768]{1,0:T(8,128)(2,1)}), bf16[3072,768]{1,0:T(8,128)(2,1)}) %all-gather.8.cloned.1.call-update) | async-done | bytes 4718608 | tf_op jit(solution)/shard_map/all_gather | solution.py:367
  157.3 5.5 %fusion.71 = f32[256,3072]{1,0:T(8,128)} fusion(bf16[256,768]{1,0:T(8,128)(2,1)} %bitcast.141, bf16[3072,768]{1,0:T(8,128)(2,1)} %all-gather.8.cloned.1.call-done), kind=kOutput, calls=%fused_computation.162 | convolution fusion | flops 1207959552 | bytes 8257536 | tf_op jit(solution)/shard_map/dot_general | solution.py:45
  163.5 2.5 slice.106
  166.4 2.8 fusion.70
  169.2 1.4 multiply_reduce_fusion.4
  170.6 54.6 %all-gather.6.cloned.1.call-done = bf16[3072,768]{1,0:T(8,128)(2,1)} async-done(((bf16[96,768]{1,0:T(8,128)(2,1)}), bf16[3072,768]{1,0:T(8,128)(2,1)}) %all-gather.6.cloned.1.call-update) | async-done | bytes 4718608 | tf_op jit(solution)/shard_map/all_gather | solution.py:366
  225.2 9.2 %fusion.65 = (bf16[3072]{0:T(1024)(128)(2,1)}, bf16[256,3072]{1,0:T(8,128)(2,1)S(1)}, f32[256,3072]{1,0:T(8,128)}) fusion(f32[256,3072]{1,0:T(8,128)} %fusion.71, f32[3072]{0:T(1024)S(1)} %add.330, bf16[3072,768]{1,0:T(8,128)(2,1)} %all-gather.6.cloned.1.call-done, f32[256,768]{1,0:T(8,128)} %get-tuple-element.80, f32[768]{0:T(1024)S(1)} %add.327, ...), kind=kOutput, calls=%fused_computation.157 | convolution fusion | flops 1226241024 | bytes 13395968 | tf_op jit(solution)/shard_map/dot_general | solution.py:45
  234.4 3.9 multiply_reduce_fusion
  238.3 1.6 fusion.68
  241.6 15.8 %all_to_all.20 = bf16[8,128,192]{1,2,0:T(8,128)(2,1)S(1)} all-to-all(bf16[8,128,192]{1,2,0:T(8,128)(2,1)S(1)} %bitcast.154), channel_id=1, replica_groups=mesh['batch'=4,'ctx'=8] {'ctx'}, dimensions={0} | all-to-all | bytes 786432 | tf_op jit(solution)/shard_map/all_to_all | solution.py:197
  257.3 1.0 copy.111
  258.3 1.0 copy-done.1
  259.4 1.0 copy-done.2
  260.4 1.2 copy-done.4
  261.7 1.0 copy-done.6
  262.7 13.1 %attention_backward.1 = bf16[1024,576]{1,0:T(8,128)(2,1)S(1)} custom-call(bf16[1024,576]{1,0:T(8,128)(2,1)S(1)} %bitcast.120, bf16[1024,576]{1,0:T(8,128)(2,1)S(1)} %bitcast.121, s32[1024,3]{1,0:T(8,128)S(1)} %copy.101.low_ref, s32[1024,1]{1,0:T(8,128)S(1)} %copy-done.1, s32[1,1024]{1,0:T(1,128)S(1)} %fusion.45.kpos_ref, f32[1024,192]{1,0:T(8,128)S(1)} %copy-done.4, ...), custom_call_target="tpu_custom_call" | custom-call | tf_op jit(solution)/shard_map/attention_backward/pallas_call | solution.py:168
  275.9 1.4 copy.113
  277.3 3.9 all-to-all-start.3
  282.2 1.4 concatenate.62
  283.6 1.4 concatenate.63
  285.0 1.4 concatenate.64
  286.4 1.4 concatenate.66
  287.8 1.5 convolution_convert_fusion.3
  289.4 5.0 %convolution_convert_fusion.1 = bf16[3072,768]{1,0:T(8,128)(2,1)} fusion(bf16[256,3072]{1,0:T(8,128)(2,1)S(1)} %copy-done.17, f32[256,768]{1,0:T(8,128)} %get-tuple-element.80, f32[768]{0:T(1024)S(1)} %copy-done.39, f32[768]{0:T(1024)S(1)} %copy-done.36, f32[256]{0:T(256)S(1)} %copy-done.44, f32[256]{0:T(256)S(1)} %copy-done.41), kind=kOutput, calls=%fused_computation.2 | convolution fusion | flops 1211301888 | bytes 7086080 | tf_op jit(solution)/shard_map/dot_general | solution.py:51
  294.4 4.5 convolution_convert_fusion
  298.9 3.8 fusion.10
  302.7 7.7 %all-to-all-done.3 = bf16[8,128,576]{1,2,0:T(8,128)(2,1)S(1)} async-done(((bf16[8,128,576]{1,2,0:T(8,128)(2,1)}), bf16[8,128,576]{1,2,0:T(8,128)(2,1)S(1)}, u32[]{:S(2)}, u32[]{:S(2)}) %all-to-all-start.3) | async-done | bytes 1179680 | tf_op jit(solution)/shard_map/all_to_all | solution.py:203
  310.5 2.2 copy.115
  313.1 2.6 convolution_convert_fusion.2
  316.1 1.8 fusion.59
  317.9 1.0 multiply_reduce_fusion.1
  318.9 1.1 add_convert_fusion
  319.9 1.4 concatenate.58
  321.3 1.3 constant_dynamic-update-slice_fusion.8
  322.6 1.4 concatenate.59
  326.2 1.3 constant_dynamic-update-slice_fusion.7
  328.7 1.3 constant_dynamic-update-slice_fusion.4
  330.0 1.3 constant_dynamic-update-slice_fusion.3
  331.3 1.3 constant_dynamic-update-slice_fusion.2
  332.6 1.3 constant_dynamic-update-slice_fusion.1
  333.9 1.4 constant_dynamic-update-slice_fusion
  335.2 1.6 copy.116
  336.8 1.6 copy.118
  339.7 3.0 pad_maximum_fusion.refs_0_
  342.8 94.1 %scatter_sum.1 = (f32[112,768]{1,0:T(8,128)S(1)}, f32[96,768]{1,0:T(8,128)S(1)}, f32[96,768]{1,0:T(8,128)S(1)}) custom-call(bf16[2,2,2,2,2,112,768]{6,5,4,3,2,1,0:T(8,128)(2,1)} %pad_maximum_fusion.refs_0_, bf16[2,2,2,2,2,96,768]{6,5,4,3,2,1,0:T(8,128)(2,1)} %bitcast.125, bf16[2,2,2,2,2,96,768]{6,5,4,3,2,1,0:T(8,128)(2,1)} %bitcast.132), custom_call_target="tpu_custom_call" | custom-call | tf_op jit(solution)/shard_map/scatter_sum/pallas_call | solution.py:301
  437.2 1.9 multiply_subtract_fusion.2
  439.1 1.6 multiply_subtract_fusion.3
  441.4 1.5 multiply_subtract_fusion
  (188 shorter events, 22.1 us)
Async XLA Ops:
  7.2 73.4 %all-gather.4.cloned.1.call-start = ((), (), s32[]{:S(2)}) async-start(), calls=%async_computation.4 | async-start | bytes 5677056 | tf_op jit(solution)/shard_map/all_gather | solution.py:365
  10.6 146.6 %all-gather.8.cloned.1.call-start = ((), (), s32[]{:S(2)}) async-start(), calls=%async_computation.6 | async-start | bytes 4866048 | tf_op jit(solution)/shard_map/all_gather | solution.py:367
  12.4 212.8 %all-gather.6.cloned.1.call-start = ((), (), s32[]{:S(2)}) async-start(), calls=%async_computation.5 | async-start | bytes 4866048 | tf_op jit(solution)/shard_map/all_gather | solution.py:366
  17.0 0.6 copy-start.45
  85.7 0.7 copy-start.28
  87.0 2.3 copy-start.10
  89.3 1.7 copy-start.20
  89.7 1.6 copy-start.22
  93.4 5.7 %copy-start.49 = (s32[2,4]{1,0:T(2,128)S(1)}, s32[2,4]{1,0:T(2,128)}, u32[]{:S(2)}) copy-start(s32[2,4]{1,0:T(2,128)} %param.20) | copy-start | bytes 100
  94.8 40.4 %all-to-all-start = ((bf16[8,128,576]{1,2,0:T(8,128)(2,1)}), bf16[8,128,576]{1,2,0:T(8,128)(2,1)}, u32[]{:S(2)}, u32[]{:S(2)}) async-start(bf16[8,128,576]{1,2,0:T(8,128)(2,1)} %bitcast.12), calls=%async_computation | async-start | bytes 2359296 | tf_op jit(solution)/shard_map/all_to_all | solution.py:197
  100.1 48.2 %copy-start = (s32[1024,1]{1,0:T(8,128)}, s32[1024,1]{1,0:T(8,128)S(1)}, u32[]{:S(2)}) copy-start(s32[1024,1]{1,0:T(8,128)S(1)} %fusion.23.qpos_ref) | copy-start | bytes 12292
  146.3 1.0 copy-start.3
  147.3 15.5 %copy-start.5 = (f32[1024,3]{1,0:T(8,128)}, f32[1024,3]{1,0:T(8,128)S(1)}, u32[]{:S(2)}) copy-start(f32[1024,3]{1,0:T(8,128)S(1)} %get-tuple-element.30.lse_ref) | copy-start | bytes 36868
  148.2 17.8 %all-to-all-start.1 = ((bf16[8,128,192]{1,2,0:T(8,128)(2,1)}), bf16[8,128,192]{1,2,0:T(8,128)(2,1)S(1)}, u32[]{:S(2)}, u32[]{:S(2)}) async-start(bf16[8,128,192]{1,2,0:T(8,128)(2,1)} %copy.102), calls=%async_computation.1 | async-start | bytes 786432 | tf_op jit(solution)/shard_map/all_to_all | solution.py:203
  157.3 5.7 %slice-start.2 = ((f32[12,32,24]{1,2,0:T(8,128)}), f32[4,32,24]{1,2,0:T(8,128)S(1)}, s32[]{:S(2)}) async-start(f32[12,32,24]{1,2,0:T(8,128)} %copy-done.28), calls=%async_computation.9 | async-start | bytes 98304 | tf_op jit(solution)/shard_map/slice | solution.py:395
  162.8 3.6 copy-start.11
  163.3 61.9 %copy-start.38 = (f32[768]{0:T(1024)}, f32[768]{0:T(1024)S(1)}, u32[]{:S(2)}) copy-start(f32[768]{0:T(1024)S(1)} %add.327) | copy-start | bytes 9220
  163.5 74.8 %copy-start.35 = (f32[768]{0:T(1024)}, f32[768]{0:T(1024)S(1)}, u32[]{:S(2)}) copy-start(f32[768]{0:T(1024)S(1)} %mul.380) | copy-start | bytes 9220
  166.4 4.2 copy-start.23
  169.2 69.1 %copy-start.40 = (f32[256]{0:T(256)}, f32[256]{0:T(256)S(1)}, u32[]{:S(2)}) copy-start(f32[256]{0:T(256)S(1)} %broadcast_multiply_fusion) | copy-start | bytes 3076
  170.6 67.7 %copy-start.43 = (f32[256]{0:T(256)}, f32[256]{0:T(256)S(1)}, u32[]{:S(2)}) copy-start(f32[256]{0:T(256)S(1)} %fusion.54) | copy-start | bytes 3076
  225.2 9.2 %copy-start.50 = (bf16[3072,768]{1,0:T(8,128)(2,1)S(1)}, bf16[3072,768]{1,0:T(8,128)(2,1)}, u32[]{:S(2)}) copy-start(bf16[3072,768]{1,0:T(8,128)(2,1)} %all-gather.6.cloned.1.call-done) | copy-start | bytes 14155780
  234.4 3.9 copy-start.16
  234.4 5.5 %copy-start.18 = (bf16[2,128,768]{2,1,0:T(8,128)(2,1)S(1)}, bf16[2,128,768]{2,1,0:T(8,128)(2,1)}, u32[]{:S(2)}) copy-start(bf16[2,128,768]{2,1,0:T(8,128)(2,1)} %param.19) | copy-start | bytes 1179652
  238.3 2.4 copy-start.14
  240.7 17.7 %copy-start.7 = (f32[256,768]{1,0:T(8,128)}, f32[256,768]{1,0:T(8,128)S(1)}, u32[]{:S(2)}) copy-start(f32[256,768]{1,0:T(8,128)S(1)} %get-tuple-element.64) | copy-start | bytes 2359300
  258.3 1.0 copy-start.1
  259.4 1.0 copy-start.2
  260.4 1.2 copy-start.4
  261.7 1.0 copy-start.6
  275.9 5.4 %copy-start.19 = (bf16[2,128,768]{2,1,0:T(8,128)(2,1)S(1)}, bf16[2,128,768]{2,1,0:T(8,128)(2,1)}, u32[]{:S(2)}) copy-start(bf16[2,128,768]{2,1,0:T(8,128)(2,1)} %param.19) | copy-start | bytes 1179652
  275.9 11.9 %copy-start.8 = (f32[256,768]{1,0:T(8,128)S(1)}, f32[256,768]{1,0:T(8,128)}, u32[]{:S(2)}) copy-start(f32[256,768]{1,0:T(8,128)} %copy-done.7) | copy-start | bytes 2359300
  275.9 11.9 %copy-start.24 = (bf16[2,128,1,12,64]{1,0,4,3,2:T(2,128)(2,1)S(1)}, bf16[2,128,1,12,64]{1,0,4,3,2:T(2,128)(2,1)}, u32[]{:S(2)}) copy-start(bf16[2,128,1,12,64]{1,0,4,3,2:T(2,128)(2,1)} %copy-done.23) | copy-start | bytes 1179652
  277.3 12.0 %copy-start.36 = (f32[768]{0:T(1024)S(1)}, f32[768]{0:T(1024)}, u32[]{:S(2)}) copy-start(f32[768]{0:T(1024)} %copy-done.35) | copy-start | bytes 9220
  277.3 12.0 %copy-start.39 = (f32[768]{0:T(1024)S(1)}, f32[768]{0:T(1024)}, u32[]{:S(2)}) copy-start(f32[768]{0:T(1024)} %copy-done.38) | copy-start | bytes 9220
  277.3 12.0 %copy-start.41 = (f32[256]{0:T(256)S(1)}, f32[256]{0:T(256)}, u32[]{:S(2)}) copy-start(f32[256]{0:T(256)} %copy-done.40) | copy-start | bytes 3076
  277.3 12.0 %copy-start.44 = (f32[256]{0:T(256)S(1)}, f32[256]{0:T(256)}, u32[]{:S(2)}) copy-start(f32[256]{0:T(256)} %copy-done.43) | copy-start | bytes 3076
  277.3 33.0 %all-to-all-start.3 = ((bf16[8,128,576]{1,2,0:T(8,128)(2,1)}), bf16[8,128,576]{1,2,0:T(8,128)(2,1)S(1)}, u32[]{:S(2)}, u32[]{:S(2)}) async-start(bf16[8,128,576]{1,2,0:T(8,128)(2,1)} %copy.113), calls=%async_computation.3 | async-start | bytes 2359296 | tf_op jit(solution)/shard_map/all_to_all | solution.py:203
  287.8 1.5 copy-start.17
  289.3 5.1 %copy-start.51 = (f32[256,3072]{1,0:T(8,128)S(1)}, f32[256,3072]{1,0:T(8,128)}, u32[]{:S(2)}) copy-start(f32[256,3072]{1,0:T(8,128)} %get-tuple-element.81) | copy-start | bytes 9437188
  289.3 9.5 %slice-start = ((s8[4718592]{0:T(1024)(128)(4,1)}), s8[4194304]{0:T(1024)(128)(4,1)S(1)}, s32[]{:S(2)}) async-start(s8[4718592]{0:T(1024)(128)(4,1)} %bitcast.138), calls=%async_computation.7 | async-start | bytes 8388608
  294.4 4.5 slice-start.1
  313.1 2.6 copy-start.12
  313.1 2.6 copy-start.13
  313.1 3.0 copy-start.21
  313.1 2.9 copy-start.42
  316.1 1.8 copy-start.46
  316.1 2.8 copy-start.9
  338.4 1.3 copy-start.15
  342.7 94.4 %copy-start.27 = (f32[72,768]{1,0:T(8,128)S(1)}, f32[72,768]{1,0:T(8,128)}, u32[]{:S(2)}) copy-start(f32[72,768]{1,0:T(8,128)} %param.21) | copy-start | bytes 663556
  342.7 94.4 %copy-start.34 = (f32[72,768]{1,0:T(8,128)S(1)}, f32[72,768]{1,0:T(8,128)}, u32[]{:S(2)}) copy-start(f32[72,768]{1,0:T(8,128)} %param.23) | copy-start | bytes 663556
  342.7 96.3 %copy-start.33 = (f32[24,768]{1,0:T(8,128)S(1)}, f32[24,768]{1,0:T(8,128)}, u32[]{:S(2)}) copy-start(f32[24,768]{1,0:T(8,128)} %param.24) | copy-start | bytes 221188
  342.7 98.0 %copy-start.37 = (f32[12,24]{1,0:T(8,128)S(1)}, f32[12,24]{1,0:T(8,128)}, u32[]{:S(2)}) copy-start(f32[12,24]{1,0:T(8,128)} %param.33) | copy-start | bytes 3460
  342.7 98.0 %copy-start.47 = (f32[12,24]{1,0:T(8,128)S(1)}, f32[12,24]{1,0:T(8,128)}, u32[]{:S(2)}) copy-start(f32[12,24]{1,0:T(8,128)} %param.35) | copy-start | bytes 3460
  342.7 98.0 %copy-start.48 = (f32[12,24]{1,0:T(8,128)S(1)}, f32[12,24]{1,0:T(8,128)}, u32[]{:S(2)}) copy-start(f32[12,24]{1,0:T(8,128)} %param.34) | copy-start | bytes 3460
  342.7 98.6 %copy-start.25 = (f32[96,768]{1,0:T(8,128)S(1)}, f32[96,768]{1,0:T(8,128)}, u32[]{:S(2)}) copy-start(f32[96,768]{1,0:T(8,128)} %param.30) | copy-start | bytes 884740
  342.8 98.6 %copy-start.26 = (f32[96,768]{1,0:T(8,128)S(1)}, f32[96,768]{1,0:T(8,128)}, u32[]{:S(2)}) copy-start(f32[96,768]{1,0:T(8,128)} %param.27) | copy-start | bytes 884740
  342.8 98.6 %copy-start.29 = (f32[96,768]{1,0:T(8,128)S(1)}, f32[96,768]{1,0:T(8,128)}, u32[]{:S(2)}) copy-start(f32[96,768]{1,0:T(8,128)} %param.32) | copy-start | bytes 884740
  342.8 98.6 %copy-start.30 = (f32[96,768]{1,0:T(8,128)S(1)}, f32[96,768]{1,0:T(8,128)}, u32[]{:S(2)}) copy-start(f32[96,768]{1,0:T(8,128)} %param.31) | copy-start | bytes 884740
  342.8 98.6 %copy-start.31 = (f32[96,768]{1,0:T(8,128)S(1)}, f32[96,768]{1,0:T(8,128)}, u32[]{:S(2)}) copy-start(f32[96,768]{1,0:T(8,128)} %param.29) | copy-start | bytes 884740
  342.8 98.6 %copy-start.32 = (f32[96,768]{1,0:T(8,128)S(1)}, f32[96,768]{1,0:T(8,128)}, u32[]{:S(2)}) copy-start(f32[96,768]{1,0:T(8,128)} %param.28) | copy-start | bytes 884740
Sparse Core Ops, SparseCore 0:
  11.6 68.9 all-gather.3
  84.2 73.0 all-gather.7
  160.9 64.2 all-gather.5
